TPU v7x, 128 devices: a whole 4x4x4 slice. The times are simulated.
128 devices in a mesh: dp: 8 (over y, core), tp: 16 (over z, x).
Axes of the slice: x: 4, y: 4, z: 4, core: 2. Of those that a mesh axis runs over, the one named last changes fastest.
Arguments:
- old_cache: bfloat16 [256, 3072, 576], P('dp', 'tp'), may hold values from -8 to 8, as said below
- lengths: int32 [256], replicated, may hold values from 384 to 3070, as said below
- new_slot: int32 [256], replicated, may hold values from 0 to 255, as said below
- queries: bfloat16 [2, 256, 128, 576], P(None, ('dp', 'tp')), may hold values from -100 to 100
- new_latent: bfloat16 [2, 256, 576], P(None, ('dp', 'tp')), may hold values from -6 to 6
- hidden: bfloat16 [2, 256, 7168], P(None, None, 'dp'), may hold values from -6 to 6
- value_up_weight: bfloat16 [128, 512, 128], P('tp'), may hold values from -1 to 1
- w_out: bfloat16 [16384, 7168], P('tp', 'dp'), may hold values from -0.046875 to 0.046875
- norm_gain: bfloat16 [7168], P('dp'), may hold values from 0.099609375 to 1.8984375
- w_gate: bfloat16 [7168, 18432], P('dp', 'tp'), may hold values from -0.0625 to 0.0625
- w_up: bfloat16 [7168, 18432], P('dp', 'tp'), may hold values from -0.0625 to 0.0625
- w_down: bfloat16 [18432, 7168], P('tp', 'dp'), may hold values from -0.046875 to 0.046875
Outputs:
- new_cache: bfloat16 [256, 3072, 576], P(('dp', 'tp'))
- layer_out: bfloat16 [2, 256, 7168], P(None, None, 'dp')
Inputs may be any that keep to these rules, and one draw needn't show every extreme that they name: A permutation. Request r moves to device new_slot[r] // 2 (dp slowest) in new group new_slot[r] // 32; exactly 4 requests of each old group go to each new group, and they take that group's slots from (r // 32) * 4 to (r // 32) * 4 + 3. `lengths`: the largest is exactly 3070. `old_cache`: rows at or past a request's length carry no meaning.
All inputs are finite; a program needn't handle non-finite values.
Results may differ from a plain program's by a relative error of at most 0.0075.
Values may be sent and summed in bfloat16 or wider, within the bound.
A program may use at most 128 MiB of HBM per device.

v0:
```python
import jax
import jax.numpy as jnp
from jax import lax
from jax.sharding import PartitionSpec as P

D = 7168


score_scale = 0.07216878364870323
norm_eps = 1e-06


def attend_blocks(query_row, key_rows, last_pos, kv_rank):
    context = key_rows.shape[0]
    raw_all = (
        jnp.einsum("hc,pc->hp", query_row, key_rows, preferred_element_type=jnp.float32)
        * score_scale
    )
    offsets = jnp.arange(context, dtype=jnp.int32)
    masked = jnp.where(offsets[None, :] <= last_pos, raw_all, -jnp.inf)
    row_max = jnp.max(masked, axis=1, keepdims=True)
    exponent = jnp.exp(masked - row_max)
    row_total = jnp.sum(exponent, axis=1, keepdims=True)
    weights = (exponent / row_total).astype(jnp.bfloat16)
    accum = jnp.dot(weights, key_rows[:, :kv_rank], preferred_element_type=jnp.float32)
    return accum.astype(jnp.bfloat16)


def normalize(rows_in, gain):
    squares = lax.psum(jnp.sum(rows_in * rows_in, axis=1), "dp")
    return (rows_in / jnp.sqrt(squares / D + norm_eps)[:, None] * gain).astype(jnp.bfloat16)


def feed_forward(normed, w_gate, w_up, w_down):
    gate_local = jnp.dot(normed, w_gate, preferred_element_type=jnp.float32)
    up_local = jnp.dot(normed, w_up, preferred_element_type=jnp.float32)
    gate_part, up_part = lax.psum((gate_local, up_local), "dp")
    hidden_act = (jax.nn.silu(gate_part) * up_part).astype(jnp.bfloat16)
    return jnp.dot(hidden_act, w_down, preferred_element_type=jnp.float32)


def tp_whole(terms):
    return lax.psum(terms, "tp")


def shards(
    old_cache,
    lengths,
    new_slot,
    queries,
    new_latent,
    hidden,
    value_up_weight,
    w_out,
    norm_gain,
    w_gate,
    w_up,
    w_down,
):
    dp_count = lax.axis_size("dp")
    tp_count = lax.axis_size("tp")
    my_group = lax.axis_index("dp")
    my_column = lax.axis_index("tp")
    group_req, piece_len, lat_width = old_cache.shape
    per_pair = group_req // dp_count
    step_count = queries.shape[0]
    req_dev = queries.shape[1]
    req_total = new_slot.shape[0]
    context = piece_len * tp_count
    kv_rank = value_up_weight.shape[1]
    everyone = jnp.arange(req_total, dtype=jnp.int32)
    new_group = new_slot // group_req
    pair_rank = new_slot % group_req - everyone // group_req * per_pair
    my_targets = lax.dynamic_slice_in_dim(
        new_group * per_pair + pair_rank, my_group * group_req, group_req
    )
    target_places = jnp.arange(group_req, dtype=jnp.int32)
    picked = jnp.sum(
        jnp.where(my_targets[None, :] == target_places[:, None], target_places[None, :], 0), axis=1
    )
    outgoing = jnp.take(old_cache, picked, axis=0)
    incoming = lax.all_to_all(outgoing, "dp", split_axis=0, concat_axis=0, tiled=True)
    arrived = lax.all_to_all(incoming, "tp", split_axis=0, concat_axis=1, tiled=True)
    source = jnp.sum(
        jnp.where(new_slot[None, :] == everyone[:, None], everyone[None, :], 0), axis=1
    )
    my_slots = (my_group * tp_count + my_column) * req_dev + jnp.arange(req_dev, dtype=jnp.int32)
    my_lengths = jnp.take(lengths, jnp.take(source, my_slots))
    positions = jnp.arange(context, dtype=jnp.int32)
    kv_cache = arrived
    for step_no in range(step_count):
        kv_cache = jnp.where(
            positions[None, :, None] == (my_lengths + step_no)[:, None, None],
            new_latent[step_no][:, None, :],
            kv_cache,
        )
    new_cache = jnp.where(
        positions[None, :, None] < (my_lengths + step_count)[:, None, None],
        kv_cache,
        jnp.zeros((), jnp.bfloat16),
    )
    gain = norm_gain.astype(jnp.float32)
    results = []
    for step_no in range(step_count):
        latent_vectors = jnp.stack(
            [
                attend_blocks(
                    queries[step_no, item], kv_cache[item], my_lengths[item] + step_no, kv_rank
                )
                for item in range(req_dev)
            ]
        )
        spread_rows = lax.all_to_all(latent_vectors, "tp", split_axis=1, concat_axis=0, tiled=True)
        expanded_values = jnp.einsum(
            "fty,typ->ftp", spread_rows, value_up_weight, preferred_element_type=jnp.float32
        )
        expanded_values = expanded_values.astype(jnp.bfloat16).reshape(group_req, -1)
        head_terms = jnp.dot(
            lax.all_gather(expanded_values, "dp", axis=0, tiled=True),
            w_out,
            preferred_element_type=jnp.float32,
        )
        residual = hidden[step_no].astype(jnp.float32)
        after_attn = residual + tp_whole(head_terms)
        normed = normalize(after_attn, gain)
        ffn_out = tp_whole(feed_forward(normed, w_gate, w_up, w_down))
        layer_row_block = (after_attn + ffn_out).astype(jnp.bfloat16)
        results.append(layer_row_block)
    return (new_cache, jnp.stack(results))


def solution(mesh):
    in_specs = (
        P("dp", "tp", None),
        P(),
        P(),
        P(None, ("dp", "tp"), None, None),
        P(None, ("dp", "tp"), None),
        P(None, None, "dp"),
        P("tp", None, None),
        P("tp", "dp"),
        P("dp"),
        P("dp", "tp"),
        P("dp", "tp"),
        P("tp", "dp"),
    )
    out_specs = (P(("dp", "tp"), None, None), P(None, None, "dp"))
    return jax.shard_map(shards, mesh=mesh, in_specs=in_specs, out_specs=out_specs, check_vma=False)
```

profile of v0, /device:TPU:1, one launch (start us, length us, event | category | flops | bytes accessed | tf_op | source)
XLA Modules:
  0.0 617.6 jit_solution(16867954963157297451)
XLA Ops:
  7.2 0.8 fusion.66
  8.0 0.1 dynamic_slice.3
  8.1 0.1 select_reduce_fusion.1
  8.2 8.2 %gather_fusion = bf16[32,192,576]{2,1,0:T(8,128)(2,1)} fusion(bf16[32,192,576]{2,1,0:T(8,128)(2,1)} %param.14, s32[1024]{0:T(1024)S(1)} %pad_clamp_fusion), kind=kCustom, calls=%fused_computation.2 | custom fusion | bytes 14155904 | tf_op jit(solution)/shard_map/jit(_take)/gather | solution.py:81
  16.5 7.2 %broadcast_select_fusion = bf16[32,192,576]{2,1,0:T(8,128)(2,1)} fusion(bf16[32,192,576]{2,1,0:T(8,128)(2,1)} %gather_fusion, pred[32]{0:T(512)(128)(4,1)S(1)} %compare_and_fusion), kind=kLoop, calls=%fused_computation.5 | loop fusion | flops 3538944 | bytes 14155808 | tf_op jit(solution)/shard_map/jit(_take)/select_n | solution.py:81
  23.7 96.2 %all_to_all.59 = bf16[32,192,576]{2,1,0:T(8,128)(2,1)} all-to-all(bf16[32,192,576]{2,1,0:T(8,128)(2,1)} %broadcast_select_fusion), channel_id=1, replica_groups=mesh['dp'=8,'tp'=16] {'dp'}, dimensions={0} | all-to-all | bytes 14155776 | tf_op jit(solution)/shard_map/all_to_all | solution.py:82
  119.9 7.9 %all-to-all-start.1 = ((bf16[32,192,576]{2,1,0:T(8,128)(2,1)}), bf16[32,192,576]{2,1,0:T(8,128)(2,1)}, u32[]{:S(2)}, u32[]{:S(2)}) async-start(bf16[32,192,576]{2,1,0:T(8,128)(2,1)} %all_to_all.59), calls=%async_computation.1 | async-start | bytes 15728640 | tf_op jit(solution)/shard_map/all_to_all | solution.py:83
  127.8 0.1 select_reduce_fusion
  127.9 0.6 gather_fusion.1
  128.6 0.6 gather_fusion.2
  129.2 0.6 fusion.76
  131.1 0.7 iota_compare_fusion.7
  131.8 0.7 iota_compare_fusion.8
  132.5 0.1 iota_compare_fusion.2
  132.6 0.1 iota_compare_fusion.1
  132.7 109.4 %all-to-all-done.1 = bf16[32,192,576]{2,1,0:T(8,128)(2,1)} async-done(((bf16[32,192,576]{2,1,0:T(8,128)(2,1)}), bf16[32,192,576]{2,1,0:T(8,128)(2,1)}, u32[]{:S(2)}, u32[]{:S(2)}) %all-to-all-start.1) | async-done | bytes 7077920 | tf_op jit(solution)/shard_map/all_to_all | solution.py:83
  242.1 7.1 %copy.31 = bf16[16,2,192,576]{3,2,0,1:T(8,128)(2,1)} copy(bf16[16,2,192,576]{3,2,1,0:T(8,128)(2,1)} %bitcast.4) | data formatting | bytes 14155776 | tf_op jit(solution)/shard_map/all_to_all | solution.py:83
  249.2 7.4 %broadcast_select_fusion.1 = (bf16[2,3072,576]{2,1,0:T(8,128)(2,1)}, bf16[2,3072,576]{2,1,0:T(8,128)(2,1)S(1)}) fusion(pred[2,3072]{1,0:T(4,128)(4,1)S(1)} %get-tuple-element.42, bf16[16,2,192,576]{3,2,0,1:T(8,128)(2,1)} %copy.31, bf16[2,576]{1,0:T(2,128)(2,1)S(1)} %get-tuple-element.30, pred[2,3072]{1,0:T(4,128)(4,1)S(1)} %get-tuple-element.41, ...), kind=kLoop, calls=%fused_computation.6 | loop fusion | flops 10616832 | bytes 21256704 | tf_op jit(solution)/shard_map/jit(_where)/select_n | solution.py:97
  256.6 0.7 slice_bitcast_fusion.1
  257.3 0.7 copy-done.19
  258.1 1.2 fusion.77
  259.3 0.4 copy-done.2
  259.7 1.2 fusion.78
  261.0 0.4 fusion.14
  261.4 0.7 fusion.32
  262.2 0.4 fusion.13
  262.6 0.7 fusion.38
  263.4 1.0 copy.32
  264.4 5.7 all-to-all-start.2
  270.0 3.9 fusion.79
  274.0 0.4 fusion.16
  274.4 0.7 fusion.29
  275.2 3.9 fusion.80
  279.1 0.4 fusion.15
  279.5 0.7 fusion.35
  280.3 1.0 copy.35
  281.3 6.7 %all-to-all-start.3 = ((bf16[2,128,512]{2,0,1:T(2,128)(2,1)}), bf16[2,128,512]{2,0,1:T(2,128)(2,1)}, u32[]{:S(2)}, u32[]{:S(2)}) async-start(bf16[2,128,512]{2,0,1:T(2,128)(2,1)} %copy.35), calls=%async_computation.3 | async-start | bytes 524288 | tf_op jit(solution)/shard_map/all_to_all | solution.py:113
  288.0 0.9 copy.46
  288.9 1.1 all_to_all.50
  290.0 0.3 fusion.41
  290.3 17.1 %all_gather.6 = bf16[256,1024]{1,0:T(8,128)(2,1)} all-gather(bf16[32,1024]{1,0:T(8,128)(2,1)S(1)} %bitcast.129), channel_id=1, replica_groups=mesh['dp'=8,'tp'=16] {'dp'}, dimensions={0}, use_global_device_ids=true | all-gather | bytes 589824 | tf_op jit(solution)/shard_map/all_gather | solution.py:119
  307.4 1.1 copy.45
  308.5 0.8 all_to_all.54
  309.3 1.4 fusion.42
  310.7 13.1 %all_gather.7 = bf16[256,1024]{1,0:T(8,128)(2,1)S(1)} all-gather(bf16[32,1024]{1,0:T(8,128)(2,1)S(1)} %bitcast.130), channel_id=1, replica_groups=mesh['dp'=8,'tp'=16] {'dp'}, dimensions={0}, use_global_device_ids=true | all-gather | bytes 589824 | tf_op jit(solution)/shard_map/all_gather | solution.py:119
  323.8 2.7 fusion.81
  326.5 1.6 fusion.82
  328.1 0.0 all-reduce.12.cloned.1.call-start
  328.2 0.6 copy-done.14
  328.8 87.3 %all-reduce.10.cloned.1.call-done = (f32[256,896]{1,0:T(8,128)}, f32[256,896]{1,0:T(8,128)}) async-done(((f32[256,896]{1,0:T(8,128)}, f32[256,896]{1,0:T(8,128)}), (f32[256,896]{1,0:T(8,128)}, f32[256,896]{1,0:T(8,128)})) %all-reduce.10.cloned.1.call-update) | async-done | bytes 1835024 | tf_op jit(solution)/shard_map/psum | solution.py:43
  416.1 1.8 multiply_reduce_fusion.1
  417.9 13.8 %all-reduce.2 = (f32[256]{0:T(256)S(1)}, f32[256]{0:T(256)S(1)}) all-reduce(f32[256]{0:T(256)S(1)} %get-tuple-element.10, f32[256]{0:T(256)S(1)} %get-tuple-element.9), channel_id=1, replica_groups=mesh['dp'=8,'tp'=16] {'dp'}, use_global_device_ids=true, to_apply=%region_18.20 | all-reduce | flops 512 | bytes 4096 | tf_op jit(solution)/shard_map/psum | solution.py:30
  431.7 3.2 fusion.73
  434.9 2.0 fusion.74
  437.0 1.9 fusion.71
  438.9 2.0 fusion.72
  440.8 0.3 all-reduce.8.cloned.1.call-start
  441.1 70.6 %all-reduce.12.cloned.1.call-done = (f32[256,1152]{1,0:T(8,128)}, f32[256,1152]{1,0:T(8,128)}, f32[256,1152]{1,0:T(8,128)}, f32[256,1152]{1,0:T(8,128)}) async-done(((f32[256,1152]{1,0:T(8,128)}, f32[256,1152]{1,0:T(8,128)}, f32[256,1152]{1,0:T(8,128)}, f32[256,1152]{1,0:T(8,128)}), (f32[256,1152]{1,0:T(8,128)}, f32[256,1152]{1,0:T(8,128)}, f32[256,1152]{1,0:T(8,128)}, ...) | async-done | bytes 4718608 | tf_op jit(solution)/shard_map/psum | solution.py:37
  511.7 4.2 fusion.52
  515.9 1.8 fusion.51
  517.7 10.1 %copy.38 = bf16[2,3072,576]{1,2,0:T(8,128)(2,1)} copy(bf16[2,3072,576]{2,1,0:T(8,128)(2,1)} %get-tuple-element.21) | data formatting | bytes 14155776
  527.8 80.0 %all-reduce.8.cloned.1.call-done = (f32[256,896]{1,0:T(8,128)}, f32[256,896]{1,0:T(8,128)}) async-done(((f32[256,896]{1,0:T(8,128)}, f32[256,896]{1,0:T(8,128)}), (f32[256,896]{1,0:T(8,128)}, f32[256,896]{1,0:T(8,128)})) %all-reduce.8.cloned.1.call-update) | async-done | bytes 1835024 | tf_op jit(solution)/shard_map/psum | solution.py:43
  607.9 2.2 fusion.55
  610.1 1.0 pad_maximum_fusion
  (62 shorter events, 0.4 us)
Async XLA Ops:
  7.2 424.5 %copy-start = (bf16[896,1152]{1,0:T(8,128)(2,1)S(1)}, bf16[896,1152]{1,0:T(8,128)(2,1)}, u32[]{:S(2)}) copy-start(bf16[896,1152]{1,0:T(8,128)(2,1)} %param.24) | copy-start | bytes 6193156
  119.9 7.9 %copy-start.13 = (s32[256]{0:T(256)S(1)}, s32[256]{0:T(256)}, u32[]{:S(2)}) copy-start(s32[256]{0:T(256)} %param.16) | copy-start | bytes 3076
  119.9 8.7 %copy-start.1 = (s32[256]{0:T(256)S(1)}, s32[256]{0:T(256)}, u32[]{:S(2)}) copy-start(s32[256]{0:T(256)} %param.15) | copy-start | bytes 3076
  119.9 12.6 %copy-start.12 = (bf16[2,2,576]{2,1,0:T(2,128)(2,1)S(1)}, bf16[2,2,576]{2,1,0:T(2,128)(2,1)}, u32[]{:S(2)}) copy-start(bf16[2,2,576]{2,1,0:T(2,128)(2,1)} %param.18) | copy-start | bytes 13828
  119.9 122.2 %all-to-all-start.1 = ((bf16[32,192,576]{2,1,0:T(8,128)(2,1)}), bf16[32,192,576]{2,1,0:T(8,128)(2,1)}, u32[]{:S(2)}, u32[]{:S(2)}) async-start(bf16[32,192,576]{2,1,0:T(8,128)(2,1)} %all_to_all.59), calls=%async_computation.1 | async-start | bytes 15728640 | tf_op jit(solution)/shard_map/all_to_all | solution.py:83
  256.6 3.1 copy-start.2
  256.6 1.5 copy-start.19
  258.1 3.3 copy-start.7
  258.1 4.5 copy-start.5
  264.4 16.9 %all-to-all-start.2 = ((bf16[2,128,512]{2,0,1:T(2,128)(2,1)}), bf16[2,128,512]{2,0,1:T(2,128)(2,1)S(1)}, u32[]{:S(2)}, u32[]{:S(2)}) async-start(bf16[2,128,512]{2,0,1:T(2,128)(2,1)} %copy.32), calls=%async_computation.2 | async-start | bytes 524288 | tf_op jit(solution)/shard_map/all_to_all | solution.py:113
  270.0 4.4 copy-start.8
  275.1 4.4 copy-start.6
  280.2 9.7 %copy-start.4 = (bf16[8,512,128]{2,1,0:T(8,128)(2,1)S(1)}, bf16[8,512,128]{2,1,0:T(8,128)(2,1)}, u32[]{:S(2)}) copy-start(bf16[8,512,128]{2,1,0:T(8,128)(2,1)} %param.20) | copy-start | bytes 3145732
  281.3 26.1 %all-to-all-start.3 = ((bf16[2,128,512]{2,0,1:T(2,128)(2,1)}), bf16[2,128,512]{2,0,1:T(2,128)(2,1)}, u32[]{:S(2)}, u32[]{:S(2)}) async-start(bf16[2,128,512]{2,0,1:T(2,128)(2,1)} %copy.35), calls=%async_computation.3 | async-start | bytes 524288 | tf_op jit(solution)/shard_map/all_to_all | solution.py:113
  288.0 128.1 %all-reduce.10.cloned.1.call-start = ((), (), s32[]{:S(2)}) async-start(), calls=%async_computation.5 | async-start | bytes 3670016 | tf_op jit(solution)/shard_map/psum | solution.py:43
  309.3 14.5 %copy-start.3 = (bf16[1024,896]{1,0:T(8,128)(2,1)S(1)}, bf16[1024,896]{1,0:T(8,128)(2,1)}, u32[]{:S(2)}) copy-start(bf16[1024,896]{1,0:T(8,128)(2,1)} %param.21) | copy-start | bytes 5505028
  328.1 0.7 copy-start.14
  328.1 88.0 %copy-start.9 = (bf16[2,256,896]{2,1,0:T(8,128)(2,1)S(1)}, bf16[2,256,896]{2,1,0:T(8,128)(2,1)}, u32[]{:S(2)}) copy-start(bf16[2,256,896]{2,1,0:T(8,128)(2,1)} %param.19) | copy-start | bytes 2752516
  328.1 183.5 %all-reduce.12.cloned.1.call-start = ((), (), s32[]{:S(2)}) async-start(), calls=%async_computation.6 | async-start | bytes 9437184 | tf_op jit(solution)/shard_map/psum | solution.py:37
  431.7 3.3 copy-start.11
  431.7 3.3 copy-start.15
  434.9 2.0 copy-start.10
  440.8 167.0 %all-reduce.8.cloned.1.call-start = ((), (), s32[]{:S(2)}) async-start(), calls=%async_computation.4 | async-start | bytes 3670016 | tf_op jit(solution)/shard_map/psum | solution.py:43
  511.7 4.2 copy-start.16
  511.7 4.2 copy-start.17
  511.7 4.2 copy-start.18
Sparse Core Ops, SparseCore 0:
  328.3 87.7 all-reduce.9
  441.0 70.6 all-reduce.11
  517.8 90.0 all-reduce.7
where the time goes:
time: 620 us; the launch traced here: 618 us
  waiting for transfers between devices  347 us (56%)
  blocking collectives  140 us (23%)
  local copies, waits for them, and re-layouts  35.9 us (6%)
  matrix products  34.2 us (6%)
  other arithmetic  24 us (4%)
  starting transfers between devices  20.6 us (3%)
  between operations  15.4 us (2%)
    psum x2, waiting for transfers between devices, tp_whole(): return lax.psum(terms, 'tp')  167 us
    all_to_all x1, waiting for transfers between devices, shards(): lax.all_to_all(incoming, 'tp', split_axis=0, concat_axis=1, tiled=True)  109 us
    all_to_all x1, blocking collectives, shards(): lax.all_to_all(outgoing, 'dp', split_axis=0, concat_axis=0, tiled=True)  96.2 us
    psum x1, waiting for transfers between devices, feed_forward(): gate_part, up_part = lax.psum((gate_local, up_local), 'dp')  70.6 us
    all_gather x2, blocking collectives, shards(): lax.all_gather(expanded_values, 'dp', axis=0, tiled=True)  30.2 us
    psum x1, blocking collectives, normalize(): squares = lax.psum(jnp.sum(rows_in * rows_in, axis=1), 'dp')  13.8 us
  transfers between devices with their start and end apart: 6, of which 4 were waited for; matrix products, arithmetic and copies ran while one was open for 4% of the time, Pallas kernels for 0%

commit v1 on v0

--- a/solution.py
+++ b/solution.py
@@ -1,9 +1,128 @@
+import functools
+
 import jax
 import jax.numpy as jnp
 from jax import lax
+from jax.experimental import pallas as pl
+from jax.experimental.pallas import tpu as pltpu
 from jax.sharding import PartitionSpec as P
 
 D = 7168
+
+
+MESH = pl.DeviceIdType.MESH
+
+
+def loop(low, high, action):
+    def body(i, carry):
+        action(i)
+        return carry
+
+    lax.fori_loop(low, high, body, 0)
+
+
+def move_kernel(n_dp, n_tp, chunks, picked, cache, out, loaded, stage, mid, load_sem, own_sem, send1, recv1, send2, recv2):
+    group_req, piece, _ = loaded.shape
+    per_pair = group_req // n_dp
+    per_dev = group_req // n_tp
+    rows = piece // chunks
+    g = lax.axis_index("dp")
+    c = lax.axis_index("tp")
+    load = pltpu.make_async_copy(cache, loaded, load_sem)
+    load.start()
+    barrier = pltpu.get_barrier_semaphore()
+
+    def greet_dp(i):
+        pl.semaphore_signal(barrier, 1, device_id=(lax.rem(g + i, n_dp), c), device_id_type=MESH)
+
+    def greet_tp(i):
+        pl.semaphore_signal(barrier, 1, device_id=(g, lax.rem(c + i, n_tp)), device_id_type=MESH)
+
+    loop(1, n_dp, greet_dp)
+    loop(1, n_tp, greet_tp)
+    pl.semaphore_wait(barrier, n_dp + n_tp - 2)
+    load.wait()
+
+    def sort(i):
+        stage[i] = loaded[picked[i]]
+
+    loop(0, group_req, sort)
+
+    def keep(i):
+        mid[per_pair * g + i] = stage[per_pair * g + i]
+
+    loop(0, per_pair, keep)
+
+    def over_dp(q, i, from_group):
+        to_group = lax.rem(g + i, n_dp)
+        part = pl.ds(q * rows, rows)
+        return pltpu.make_async_remote_copy(
+            src_ref=stage.at[pl.ds(per_pair * to_group, per_pair), part],
+            dst_ref=mid.at[pl.ds(per_pair * from_group, per_pair), part],
+            send_sem=send1.at[q, to_group],
+            recv_sem=recv1.at[q, from_group],
+            device_id=(to_group, c),
+            device_id_type=MESH,
+        )
+
+    def over_tp(q, i, from_column):
+        to_column = lax.rem(c + i, n_tp)
+        return pltpu.make_async_remote_copy(
+            src_ref=mid.at[pl.ds(per_dev * to_column, per_dev), pl.ds(q * rows, rows)],
+            dst_ref=out.at[:, pl.ds(from_column * piece + q * rows, rows)],
+            send_sem=send2.at[q, to_column],
+            recv_sem=recv2.at[q, from_column],
+            device_id=(g, to_column),
+            device_id_type=MESH,
+        )
+
+    def own(q):
+        return pltpu.make_async_copy(
+            mid.at[pl.ds(per_dev * c, per_dev), pl.ds(q * rows, rows)],
+            out.at[:, pl.ds(c * piece + q * rows, rows)],
+            own_sem.at[q],
+        )
+
+    ahead = 2
+    for q in range(chunks + 1):
+        if q < chunks:
+            if q >= ahead:
+                loop(1, n_dp, lambda i: over_dp(q - ahead, i, g).wait_send())
+            loop(1, n_dp, lambda i: over_dp(q, i, g).start())
+        if q >= 1:
+            loop(1, n_dp, lambda i: over_dp(q - 1, i, lax.rem(g + n_dp - i, n_dp)).wait_recv())
+            loop(1, n_tp, lambda i: over_tp(q - 1, i, c).start())
+            own(q - 1).start()
+    for q in range(chunks):
+        if q >= chunks - ahead:
+            loop(1, n_dp, lambda i: over_dp(q, i, g).wait_send())
+        loop(1, n_tp, lambda i: over_tp(q, i, c).wait_send())
+        loop(1, n_tp, lambda i: over_tp(q, i, lax.rem(c + n_tp - i, n_tp)).wait_recv())
+        own(q).wait()
+
+
+def move(picked, old_cache, n_dp, n_tp):
+    group_req, piece, width = old_cache.shape
+    chunks = 12
+    sems = pltpu.SemaphoreType.DMA
+    return pl.pallas_call(
+        functools.partial(move_kernel, n_dp, n_tp, chunks),
+        out_shape=jax.ShapeDtypeStruct((group_req // n_tp, piece * n_tp, width), old_cache.dtype),
+        in_specs=[pl.BlockSpec(memory_space=pltpu.SMEM), pl.BlockSpec(memory_space=pl.ANY)],
+        out_specs=pl.BlockSpec(memory_space=pl.ANY),
+        scratch_shapes=[
+            pltpu.VMEM(old_cache.shape, old_cache.dtype),
+            pltpu.VMEM(old_cache.shape, old_cache.dtype),
+            pltpu.VMEM(old_cache.shape, old_cache.dtype),
+            sems,
+            sems((chunks,)),
+            sems((chunks, n_dp)),
+            sems((chunks, n_dp)),
+            sems((chunks, n_tp)),
+            sems((chunks, n_tp)),
+        ],
+        compiler_params=pltpu.CompilerParams(collective_id=0, has_side_effects=True, vmem_limit_bytes=48 * 2**20),
+    )(picked, old_cache)
 
 
 score_scale = 0.07216878364870323
@@ -78,9 +197,7 @@
     picked = jnp.sum(
         jnp.where(my_targets[None, :] == target_places[:, None], target_places[None, :], 0), axis=1
     )
-    outgoing = jnp.take(old_cache, picked, axis=0)
-    incoming = lax.all_to_all(outgoing, "dp", split_axis=0, concat_axis=0, tiled=True)
-    arrived = lax.all_to_all(incoming, "tp", split_axis=0, concat_axis=1, tiled=True)
+    arrived = move(picked, old_cache, dp_count, tp_count)
     source = jnp.sum(
         jnp.where(new_slot[None, :] == everyone[:, None], everyone[None, :], 0), axis=1
     )

time: 620 us -> 495 us (0.80)
  Pallas kernels: 0 us -> 113 us
  waiting for transfers between devices: 347 us -> 238 us
  blocking collectives: 140 us -> 42.2 us
  local copies, waits for them, and re-layouts: 35.9 us -> 20.8 us
  starting transfers between devices: 20.6 us -> 12.4 us
  other arithmetic: 24 us -> 17.5 us
    pallas_call x0 -> x1, Pallas kernels: none -> 113 us  [move(): pl.pallas_call(functools.partial(move_kernel, n_dp, n_tp, chunks), out_sh...]
    all_to_all x1 -> x0, waiting for transfers between devices: 109 us -> none  [shards(): lax.all_to_all(incoming, 'tp', split_axis=0, concat_axis=1, tiled=True)]
    all_to_all x1 -> x0, blocking collectives: 96.2 us -> none  [shards(): lax.all_to_all(outgoing, 'dp', split_axis=0, concat_axis=0, tiled=True)]
    gather x1 -> x0, local copies, waits for them, and re-layouts: 8.23 us -> none  [shards(): outgoing = jnp.take(old_cache, picked, axis=0)]
    all_to_all x1 -> x0, starting transfers between devices: 7.86 us -> none  [shards(): lax.all_to_all(incoming, 'tp', split_axis=0, concat_axis=1, tiled=True)]
    select_n x2 -> x0, other arithmetic: 7.18 us -> none  [shards(): outgoing = jnp.take(old_cache, picked, axis=0)]
    all_to_all x1 -> x0, local copies, waits for them, and re-layouts: 7.14 us -> none  [shards(): lax.all_to_all(incoming, 'tp', split_axis=0, concat_axis=1, tiled=True)]
  transfers between devices with their start and end apart: 6 -> 5, of which waited for: 4 -> 3; matrix products, arithmetic and copies ran while one was open for 4% -> 5% of each run, Pallas kernels for 0% -> 0%
where the time goes in v1:
time: 495 us; the launch traced here: 493 us
  waiting for transfers between devices  238 us (48%)
  Pallas kernels  113 us (23%)
  blocking collectives  42.2 us (9%)
  matrix products  34.2 us (7%)
  local copies, waits for them, and re-layouts  20.8 us (4%)
  other arithmetic  17.5 us (4%)
  between operations  15.3 us (3%)
  starting transfers between devices  12.4 us (3%)
    psum x2, waiting for transfers between devices, tp_whole(): return lax.psum(terms, 'tp')  167 us
    pallas_call x1, Pallas kernels, move(): pl.pallas_call(functools.partial(move_kernel, n_dp, n_tp, chunks), out_sh...  113 us
    psum x1, waiting for transfers between devices, feed_forward(): gate_part, up_part = lax.psum((gate_local, up_local), 'dp')  70.5 us
    all_gather x2, blocking collectives, shards(): lax.all_gather(expanded_values, 'dp', axis=0, tiled=True)  28.4 us
    psum x1, blocking collectives, normalize(): squares = lax.psum(jnp.sum(rows_in * rows_in, axis=1), 'dp')  13.8 us
    all_to_all x2, starting transfers between devices, shards(): lax.all_to_all(latent_vectors, 'tp', split_axis=1, concat_axis=0, tiled=T...  12.1 us
    unnamed x35, local copies, waits for them, and re-layouts  10.8 us
    dot_general x4, matrix products, attend_blocks(): jnp.einsum('hc,pc->hp', query_row, key_rows, preferred_element_type=jnp.f...  10.4 us
  transfers between devices with their start and end apart: 5, of which 3 were waited for; matrix products, arithmetic and copies ran while one was open for 5% of the time, Pallas kernels for 0%

profile of v1, /device:TPU:1, one launch (start us, length us, event | category | flops | bytes accessed | tf_op | source)
XLA Modules:
  0.0 493.1 jit_solution(1753939309905982541)
XLA Ops:
  7.2 0.0 copy-start
  7.2 0.9 select_reduce_fusion
  8.1 0.7 fusion.65
  8.8 0.6 gather_fusion
  9.5 1.3 gather_fusion.1
  10.8 0.6 fusion.73
  11.5 0.1 iota_compare_fusion.1
  11.6 0.1 dynamic_slice.3
  11.7 0.1 select_reduce_fusion.1.picked
  11.8 0.7 slice_bitcast_fusion.3
  12.5 0.1 iota_compare_fusion.2
  12.6 112.7 %shard_map.131 = bf16[2,3072,576]{2,1,0:T(8,128)(2,1)} custom-call(s32[32]{0:T(128)S(1)} %select_reduce_fusion.1.picked, bf16[32,192,576]{2,1,0:T(8,128)(2,1)} %cache.1), custom_call_target="tpu_custom_call" | custom-call | tf_op jit(solution)/shard_map/pallas_call | solution.py:108
  125.3 7.4 %broadcast_select_fusion = (bf16[2,3072,576]{2,1,0:T(8,128)(2,1)}, bf16[2,3072,576]{2,1,0:T(8,128)(2,1)S(1)}) fusion(pred[2,3072]{1,0:T(4,128)(4,1)S(1)} %get-tuple-element.44, bf16[2,3072,576]{2,1,0:T(8,128)(2,1)} %shard_map.131, bf16[2,576]{1,0:T(2,128)(2,1)S(1)} %get-tuple-element.32, pred[2,3072]{1,0:T(4,128)(4,1)S(1)} %get-tuple-element.43, ...), kind=kLoop, calls=%fused_computation.3 | loop fusion | flops 10616832 | bytes 21256704 | tf_op jit(solution)/shard_map/jit(_where)/select_n | solution.py:214
  132.8 0.7 slice_bitcast_fusion.1
  133.5 0.6 iota_compare_fusion.7
  134.2 0.7 iota_compare_fusion.8
  134.8 1.2 fusion.74
  136.1 1.2 fusion.75
  137.3 0.4 fusion.13
  137.7 0.7 fusion.31
  138.5 0.4 fusion.12
  138.9 0.7 fusion.37
  139.7 1.0 copy.29
  140.7 5.4 %all-to-all-start = ((bf16[2,128,512]{2,0,1:T(2,128)(2,1)}), bf16[2,128,512]{2,0,1:T(2,128)(2,1)S(1)}, u32[]{:S(2)}, u32[]{:S(2)}) async-start(bf16[2,128,512]{2,0,1:T(2,128)(2,1)} %copy.29), calls=%async_computation | async-start | bytes 524288 | tf_op jit(solution)/shard_map/all_to_all | solution.py:230
  147.3 3.9 fusion.76
  151.3 0.4 fusion.15
  151.7 0.7 fusion.28
  152.5 3.9 fusion.77
  156.4 0.4 fusion.14
  156.9 0.7 fusion.34
  157.6 0.0 copy-start.3
  157.6 1.0 copy.32
  158.6 6.7 %all-to-all-start.1 = ((bf16[2,128,512]{2,0,1:T(2,128)(2,1)}), bf16[2,128,512]{2,0,1:T(2,128)(2,1)}, u32[]{:S(2)}, u32[]{:S(2)}) async-start(bf16[2,128,512]{2,0,1:T(2,128)(2,1)} %copy.32), calls=%async_computation.1 | async-start | bytes 524288 | tf_op jit(solution)/shard_map/all_to_all | solution.py:230
  165.3 0.0 all-reduce.10.cloned.1.call-start
  165.4 0.9 copy.43
  166.3 1.1 all_to_all.29
  167.3 0.3 fusion.40
  167.6 15.3 %all_gather.6 = bf16[256,1024]{1,0:T(8,128)(2,1)} all-gather(bf16[32,1024]{1,0:T(8,128)(2,1)S(1)} %bitcast.117), channel_id=1, replica_groups=mesh['dp'=8,'tp'=16] {'dp'}, dimensions={0}, use_global_device_ids=true | all-gather | bytes 589824 | tf_op jit(solution)/shard_map/all_gather | solution.py:236
  182.9 1.1 copy.42
  184.1 0.8 all_to_all.33
  184.9 1.4 fusion.41
  186.3 13.1 %all_gather.7 = bf16[256,1024]{1,0:T(8,128)(2,1)S(1)} all-gather(bf16[32,1024]{1,0:T(8,128)(2,1)S(1)} %bitcast.118), channel_id=1, replica_groups=mesh['dp'=8,'tp'=16] {'dp'}, dimensions={0}, use_global_device_ids=true | all-gather | bytes 589824 | tf_op jit(solution)/shard_map/all_gather | solution.py:236
  199.4 2.7 fusion.78
  202.0 1.6 fusion.79
  203.7 0.0 all-reduce.10.cloned.1.call-update
  203.7 0.0 all-reduce.12.cloned.1.call-start
  203.8 0.6 copy-done.11
  204.4 87.3 %all-reduce.10.cloned.1.call-done = (f32[256,896]{1,0:T(8,128)}, f32[256,896]{1,0:T(8,128)}) async-done(((f32[256,896]{1,0:T(8,128)}, f32[256,896]{1,0:T(8,128)}), (f32[256,896]{1,0:T(8,128)}, f32[256,896]{1,0:T(8,128)})) %all-reduce.10.cloned.1.call-update) | async-done | bytes 1835024 | tf_op jit(solution)/shard_map/psum | solution.py:162
  291.7 1.8 multiply_reduce_fusion.1
  293.4 13.8 %all-reduce.2 = (f32[256]{0:T(256)S(1)}, f32[256]{0:T(256)S(1)}) all-reduce(f32[256]{0:T(256)S(1)} %get-tuple-element.12, f32[256]{0:T(256)S(1)} %get-tuple-element.11), channel_id=1, replica_groups=mesh['dp'=8,'tp'=16] {'dp'}, use_global_device_ids=true, to_apply=%region_18.20 | all-reduce | flops 512 | bytes 4096 | tf_op jit(solution)/shard_map/psum | solution.py:149
  307.3 3.2 fusion.71
  310.5 2.0 fusion.72
  312.5 1.9 fusion.69
  314.4 1.9 fusion.70
  316.3 0.0 all-reduce.12.cloned.1.call-update
  316.3 0.3 all-reduce.8.cloned.1.call-start
  316.6 70.5 %all-reduce.12.cloned.1.call-done = (f32[256,1152]{1,0:T(8,128)}, f32[256,1152]{1,0:T(8,128)}, f32[256,1152]{1,0:T(8,128)}, f32[256,1152]{1,0:T(8,128)}) async-done(((f32[256,1152]{1,0:T(8,128)}, f32[256,1152]{1,0:T(8,128)}, f32[256,1152]{1,0:T(8,128)}, f32[256,1152]{1,0:T(8,128)}), (f32[256,1152]{1,0:T(8,128)}, f32[256,1152]{1,0:T(8,128)}, f32[256,1152]{1,0:T(8,128)}, ...) | async-done | bytes 4718608 | tf_op jit(solution)/shard_map/psum | solution.py:156
  387.1 4.2 fusion.51
  391.3 1.8 fusion.50
  393.1 0.0 all-reduce.8.cloned.1.call-update
  393.2 10.1 %copy.35 = bf16[2,3072,576]{1,2,0:T(8,128)(2,1)} copy(bf16[2,3072,576]{2,1,0:T(8,128)(2,1)} %get-tuple-element.23) | data formatting | bytes 14155776
  403.3 80.0 %all-reduce.8.cloned.1.call-done = (f32[256,896]{1,0:T(8,128)}, f32[256,896]{1,0:T(8,128)}) async-done(((f32[256,896]{1,0:T(8,128)}, f32[256,896]{1,0:T(8,128)}), (f32[256,896]{1,0:T(8,128)}, f32[256,896]{1,0:T(8,128)})) %all-reduce.8.cloned.1.call-update) | async-done | bytes 1835024 | tf_op jit(solution)/shard_map/psum | solution.py:162
  483.3 2.2 fusion.54
  485.6 1.0 pad_maximum_fusion
  (48 shorter events, 0.3 us)
Async XLA Ops:
  7.2 300.1 %copy-start = (bf16[896,1152]{1,0:T(8,128)(2,1)S(1)}, bf16[896,1152]{1,0:T(8,128)(2,1)}, u32[]{:S(2)}) copy-start(bf16[896,1152]{1,0:T(8,128)(2,1)} %param.24) | copy-start | bytes 6193156
  132.7 3.3 copy-start.1
  132.8 2.1 copy-start.16
  133.5 4.3 copy-start.6
  133.5 5.4 %copy-start.4 = (bf16[3072,576]{1,0:T(8,128)(2,1)}, bf16[3072,576]{1,0:T(8,128)(2,1)S(1)}, u32[]{:S(2)}) copy-start(bf16[3072,576]{1,0:T(8,128)(2,1)S(1)} %get-tuple-element.27) | copy-start | bytes 10616836
  140.7 17.9 %all-to-all-start = ((bf16[2,128,512]{2,0,1:T(2,128)(2,1)}), bf16[2,128,512]{2,0,1:T(2,128)(2,1)S(1)}, u32[]{:S(2)}, u32[]{:S(2)}) async-start(bf16[2,128,512]{2,0,1:T(2,128)(2,1)} %copy.29), calls=%async_computation | async-start | bytes 524288 | tf_op jit(solution)/shard_map/all_to_all | solution.py:230
  147.3 4.4 copy-start.7
  152.5 4.4 copy-start.5
  157.6 9.8 %copy-start.3 = (bf16[8,512,128]{2,1,0:T(8,128)(2,1)S(1)}, bf16[8,512,128]{2,1,0:T(8,128)(2,1)}, u32[]{:S(2)}) copy-start(bf16[8,512,128]{2,1,0:T(8,128)(2,1)} %param.20) | copy-start | bytes 3145732
  158.6 24.3 %all-to-all-start.1 = ((bf16[2,128,512]{2,0,1:T(2,128)(2,1)}), bf16[2,128,512]{2,0,1:T(2,128)(2,1)}, u32[]{:S(2)}, u32[]{:S(2)}) async-start(bf16[2,128,512]{2,0,1:T(2,128)(2,1)} %copy.32), calls=%async_computation.1 | async-start | bytes 524288 | tf_op jit(solution)/shard_map/all_to_all | solution.py:230
  165.3 126.4 %all-reduce.10.cloned.1.call-start = ((), (), s32[]{:S(2)}) async-start(), calls=%async_computation.3 | async-start | bytes 3670016 | tf_op jit(solution)/shard_map/psum | solution.py:162
  184.9 14.5 %copy-start.2 = (bf16[1024,896]{1,0:T(8,128)(2,1)S(1)}, bf16[1024,896]{1,0:T(8,128)(2,1)}, u32[]{:S(2)}) copy-start(bf16[1024,896]{1,0:T(8,128)(2,1)} %param.21) | copy-start | bytes 5505028
  203.7 0.7 copy-start.11
  203.7 88.0 %copy-start.8 = (bf16[2,256,896]{2,1,0:T(8,128)(2,1)S(1)}, bf16[2,256,896]{2,1,0:T(8,128)(2,1)}, u32[]{:S(2)}) copy-start(bf16[2,256,896]{2,1,0:T(8,128)(2,1)} %param.19) | copy-start | bytes 2752516
  203.7 183.4 %all-reduce.12.cloned.1.call-start = ((), (), s32[]{:S(2)}) async-start(), calls=%async_computation.4 | async-start | bytes 9437184 | tf_op jit(solution)/shard_map/psum | solution.py:156
  307.3 3.3 copy-start.10
  307.3 3.3 copy-start.12
  310.5 2.0 copy-start.9
  316.3 167.0 %all-reduce.8.cloned.1.call-start = ((), (), s32[]{:S(2)}) async-start(), calls=%async_computation.2 | async-start | bytes 3670016 | tf_op jit(solution)/shard_map/psum | solution.py:162
  387.1 4.2 copy-start.13
  387.1 4.2 copy-start.14
  387.1 4.2 copy-start.15
Sparse Core Ops, SparseCore 0:
  203.8 87.7 all-reduce.9
  316.4 70.6 all-reduce.11
  393.3 90.0 all-reduce.7

commit v2 on v1

--- a/solution.py
+++ b/solution.py
@@ -145,21 +145,338 @@
     return accum.astype(jnp.bfloat16)
 
 
-def normalize(rows_in, gain):
-    squares = lax.psum(jnp.sum(rows_in * rows_in, axis=1), "dp")
-    return (rows_in / jnp.sqrt(squares / D + norm_eps)[:, None] * gain).astype(jnp.bfloat16)
-
-
-def feed_forward(normed, w_gate, w_up, w_down):
-    gate_local = jnp.dot(normed, w_gate, preferred_element_type=jnp.float32)
-    up_local = jnp.dot(normed, w_up, preferred_element_type=jnp.float32)
-    gate_part, up_part = lax.psum((gate_local, up_local), "dp")
-    hidden_act = (jax.nn.silu(gate_part) * up_part).astype(jnp.bfloat16)
-    return jnp.dot(hidden_act, w_down, preferred_element_type=jnp.float32)
-
-
-def tp_whole(terms):
-    return lax.psum(terms, "tp")
+def dense_kernel(
+    lat,
+    value_up,
+    hidden,
+    gain,
+    w_out,
+    w_gate,
+    w_up,
+    w_down,
+    out,
+    vup_v,
+    wout_v,
+    wgate_v,
+    wup_v,
+    wdown_v,
+    latr,
+    perm,
+    xbuf,
+    s3,
+    r3,
+    after,
+    ybuf,
+    gu,
+    keep,
+    pair_s,
+    pair_r,
+    ring_s,
+    ring_r,
+    hbuf,
+    wsem,
+    lat_ss,
+    lat_rs,
+    x_ss,
+    x_rs,
+    s3_ss,
+    s3_rs,
+    y_ss,
+    y_rs,
+    pair_ss,
+    pair_rs,
+    ring_ss,
+    ring_rs,
+    h_ss,
+    h_rs,
+    s7_ss,
+    s7_rs,
+    o_ss,
+    o_rs,
+):
+    f32, bf16 = jnp.float32, jnp.bfloat16
+    g = lax.axis_index("dp")
+    c = lax.axis_index("tp")
+    y, k = g // 2, lax.rem(g, 2)
+    z, x = c // 4, lax.rem(c, 4)
+    sib = g + 1 - 2 * k
+    ff = wgate_v.shape[1]
+    width = 2 * ff
+
+    def owner(block):
+        return 4 * lax.rem(block, 4) + lax.rem(lax.rem(block, 4) + block // 4, 4)
+
+    mine = 4 * lax.rem(x - z + 4, 4) + z
+
+    loads = []
+    for n, (src, dst) in enumerate(
+        ((value_up, vup_v), (w_out, wout_v), (w_gate, wgate_v), (w_up, wup_v), (w_down, wdown_v))
+    ):
+        loads.append(pltpu.make_async_copy(src, dst, wsem.at[n]))
+        loads[-1].start()
+
+    def remote(src, dst, send_sem, recv_sem, dp, tp):
+        return pltpu.make_async_remote_copy(
+            src_ref=src, dst_ref=dst, send_sem=send_sem, recv_sem=recv_sem, device_id=(dp, tp), device_id_type=MESH
+        )
+
+    barrier = pltpu.get_barrier_semaphore()
+    loop(1, 16, lambda i: pl.semaphore_signal(barrier, 1, device_id=(g, lax.rem(c + i, 16)), device_id_type=MESH))
+    loop(1, 4, lambda i: pl.semaphore_signal(barrier, 1, device_id=(lax.rem(g + 2 * i, 8), c), device_id_type=MESH))
+    pl.semaphore_signal(barrier, 1, device_id=(sib, c), device_id_type=MESH)
+    pl.semaphore_wait(barrier, 19)
+
+    def lat_copy(i, source):
+        to = lax.rem(c + i, 16)
+        return remote(lat.at[to], latr.at[source], lat_ss.at[to], lat_rs.at[source], g, to)
+
+    loop(1, 16, lambda i: lat_copy(i, c).start())
+    latr[c] = lat[c]
+    row = lax.broadcasted_iota(jnp.int32, (512, 512), 0)
+    col = lax.broadcasted_iota(jnp.int32, (512, 512), 1)
+    wanted = ((row & 31) >> 1) * 32 + (row & 1) * 16 + ((row >> 5) & 1) * 8 + (row >> 6)
+    perm[...] = jnp.where(col == wanted, 1.0, 0.0).astype(bf16)
+    loop(1, 16, lambda i: lat_copy(i, lax.rem(c + 16 - i, 16)).wait_recv())
+    ordered = jnp.dot(perm[...], latr[...].reshape(512, 512), preferred_element_type=f32).astype(bf16)
+    loads[0].wait()
+    for head in range(8):
+        part = jnp.dot(ordered[64 * head : 64 * head + 64], vup_v[head], preferred_element_type=f32)
+        xbuf[g, :, 128 * head : 128 * head + 128] = part.astype(bf16)
+
+    def gather_ring(buf, ss, rs, i, source):
+        to = lax.rem(g + 2 * i, 8)
+        return remote(buf.at[g], buf.at[source], ss.at[i], rs.at[source], to, c)
+
+    def gather_pair(buf, ss, rs, i, sent, got):
+        return remote(buf.at[sent], buf.at[got], ss.at[4 + i], rs.at[got], sib, c)
+
+    def gather_start(buf, ss, rs):
+        loop(1, 4, lambda i: gather_ring(buf, ss, rs, i, g).start())
+        gather_pair(buf, ss, rs, 0, g, g).start()
+
+    def gather_step(buf, ss, rs, i):
+        src = lax.rem(g + 8 - 2 * i, 8)
+        other = src + 1 - 2 * k
+
+        @pl.when(i > 0)
+        def _():
+            gather_ring(buf, ss, rs, i, src).wait_recv()
+            gather_pair(buf, ss, rs, i, src, src).start()
+
+        gather_pair(buf, ss, rs, i, src, other).wait_recv()
+        return src // 2
+
+    def gather_end(buf, ss, rs):
+        loop(1, 4, lambda i: gather_ring(buf, ss, rs, i, g).wait_send())
+        loop(0, 4, lambda i: gather_pair(buf, ss, rs, i, g, g).wait_send())
+
+    def scatter_copy(ss, rs, block, source):
+        return remote(s3.at[block], r3.at[source], ss.at[block], rs.at[source], g, owner(block))
+
+    def scatter(value, chunk, ss, rs):
+        for j in range(4):
+            s3[4 * chunk + j] = value[32 * j : 32 * j + 32].astype(bf16)
+        for j in range(4):
+            block = 4 * chunk + j
+
+            @pl.when(block != mine)
+            def _():
+                scatter_copy(ss, rs, block, c).start()
+
+    def scatter_sum(ss, rs, first):
+        total = first
+        loop(1, 16, lambda i: scatter_copy(ss, rs, mine, lax.rem(c + 16 - i, 16)).wait_recv())
+        r3[c] = s3[mine]
+        total = total + jnp.sum(r3[...].astype(f32), axis=0)
+        def sent(i):
+            @pl.when(i != mine)
+            def _():
+                scatter_copy(ss, rs, i, c).wait_send()
+        loop(0, 16, sent)
+        return total
+
+    gather_start(xbuf, x_ss, x_rs)
+    loads[1].wait()
+
+    def out_step(i):
+        chunk = gather_step(xbuf, x_ss, x_rs, i)
+        rows = xbuf[pl.ds(2 * chunk, 2)].reshape(128, 1024)
+        scatter(jnp.dot(rows, wout_v[...], preferred_element_type=f32), chunk, s3_ss, s3_rs)
+
+    loop(0, 4, out_step)
+    residual = hidden[lax.rem(mine, 2), mine // 2].astype(f32)
+    after[...] = scatter_sum(s3_ss, s3_rs, residual)
+    gather_end(xbuf, x_ss, x_rs)
+
+    ybuf[mine] = after[...].astype(bf16)
+
+    def spread(buf_at, ss, rs, i, block):
+        to = lax.rem(c + i, 16)
+        return remote(buf_at(mine), buf_at(block), ss.at[to], rs.at[block], g, to)
+
+    def y_at(block):
+        return ybuf.at[block]
+
+    loop(1, 16, lambda i: spread(y_at, y_ss, y_rs, i, mine).start())
+    loads[2].wait()
+    loads[3].wait()
+    lane = lax.broadcasted_iota(jnp.int32, (64, 128), 1)
+
+    def two_part(total):
+        high = total.astype(bf16)
+        low = (total - high.astype(f32)).astype(bf16)
+        return jnp.where(lane < 64, high.astype(f32), low.astype(f32)).astype(bf16)
+
+    def one_part(pair):
+        return pair[:, 0:1].astype(f32) + pair[:, 64:65].astype(f32)
+
+    def pair_copy(chunk):
+        return remote(pair_s.at[chunk], pair_r.at[chunk], pair_ss.at[chunk], pair_rs.at[chunk], sib, c)
+
+    def ring_copy(chunk, source):
+        return remote(ring_s.at[chunk], ring_r.at[source], ring_ss.at[chunk], ring_rs.at[source], 2 * chunk + k, c)
+
+    def gate_step(i):
+        chunk = lax.rem(y + 1 + i, 4)
+        for j in range(4):
+            block = 4 * chunk + j
+
+            @pl.when(block != mine)
+            def _():
+                spread(y_at, y_ss, y_rs, 1, block).wait_recv()
+
+        rows = ybuf[pl.ds(4 * chunk, 4)].reshape(128, ybuf.shape[2]).astype(f32)
+        squares = jnp.sum(rows * rows, axis=1, keepdims=True)
+        scaled = (rows * gain[...]).astype(bf16)
+        gu[:, :, 0:ff] = jnp.dot(scaled, wgate_v[...], preferred_element_type=f32).reshape(2, 64, ff)
+        gu[:, :, ff:width] = jnp.dot(scaled, wup_v[...], preferred_element_type=f32).reshape(2, 64, ff)
+        gu[:, :, width : width + 128] = jnp.broadcast_to(squares, (128, 128)).reshape(2, 64, 128)
+        pair_s[chunk, :, 0:width] = gu[1 - k, :, 0:width].astype(bf16)
+        pair_s[chunk, :, width : width + 128] = two_part(gu[1 - k, :, width : width + 128])
+        pair_copy(chunk).start()
+        keep[chunk] = gu[k]
+
+    def merge_step(i):
+        chunk = lax.rem(y + 1 + i, 4)
+        pair_copy(chunk).wait_recv()
+        keep[chunk, :, 0:width] += pair_r[chunk, :, 0:width].astype(f32)
+        keep[chunk, :, width : width + 128] += one_part(pair_r[chunk, :, width : width + 128])
+
+        @pl.when(chunk != y)
+        def _():
+            ring_s[chunk, :, 0:width] = keep[chunk, :, 0:width].astype(bf16)
+            ring_s[chunk, :, width : width + 128] = two_part(keep[chunk, :, width : width + 128])
+            ring_copy(chunk, y).start()
+
+    def gate_loop(i):
+        @pl.when(i < 4)
+        def _():
+            gate_step(i)
+
+        @pl.when(i > 0)
+        def _():
+            merge_step(i - 1)
+
+    loop(0, 5, gate_loop)
+
+    def ring_add(i):
+        source = lax.rem(y + i, 4)
+        ring_copy(source, source).wait_recv()
+        keep[y, :, 0:width] += ring_r[source, :, 0:width].astype(f32)
+        keep[y, :, width : width + 128] += one_part(ring_r[source, :, width : width + 128])
+
+    loop(1, 4, ring_add)
+    squares = keep[y, :, width : width + 1]
+    scale = 1.0 / jnp.sqrt(squares / D + norm_eps)
+    gate = keep[y, :, 0:ff] * scale
+    up = keep[y, :, ff:width] * scale
+    hbuf[g] = (jax.nn.silu(gate) * up).astype(bf16)
+    gather_start(hbuf, h_ss, h_rs)
+    loads[4].wait()
+
+    def down_step(i):
+        chunk = gather_step(hbuf, h_ss, h_rs, i)
+        rows = hbuf[pl.ds(2 * chunk, 2)].reshape(128, ff)
+        scatter(jnp.dot(rows, wdown_v[...], preferred_element_type=f32), chunk, s7_ss, s7_rs)
+
+    loop(0, 4, down_step)
+    result = scatter_sum(s7_ss, s7_rs, after[...])
+    step, group = lax.rem(mine, 2), mine // 2
+    out[step, group] = result.astype(bf16)
+
+    def o_at(block):
+        return out.at[lax.rem(block, 2), block // 2]
+
+    loop(1, 16, lambda i: spread(o_at, o_ss, o_rs, i, mine).start())
+    gather_end(hbuf, h_ss, h_rs)
+    loop(1, 16, lambda i: lat_copy(i, c).wait_send())
+    loop(1, 16, lambda i: spread(y_at, y_ss, y_rs, i, mine).wait_send())
+    loop(0, 4, lambda i: pair_copy(i).wait_send())
+    loop(1, 4, lambda i: ring_copy(lax.rem(y + i, 4), y).wait_send())
+
+    def finish(block):
+        @pl.when(block != mine)
+        def _():
+            spread(o_at, o_ss, o_rs, 1, block).wait_recv()
+
+    loop(0, 16, finish)
+    loop(1, 16, lambda i: spread(o_at, o_ss, o_rs, i, mine).wait_send())
+
+
+def dense(lat, value_up, hidden, gain, w_out, w_gate, w_up, w_down):
+    steps, total, cols = hidden.shape
+    ff = w_gate.shape[1]
+    bf16, f32 = jnp.bfloat16, jnp.float32
+    vmem, sems = pltpu.VMEM, pltpu.SemaphoreType.DMA
+    in_vmem, anywhere = pl.BlockSpec(memory_space=pltpu.VMEM), pl.BlockSpec(memory_space=pl.ANY)
+    result = pl.pallas_call(
+        dense_kernel,
+        out_shape=jax.ShapeDtypeStruct((steps, 8, 32, cols), bf16),
+        in_specs=[in_vmem, anywhere, in_vmem, in_vmem, anywhere, anywhere, anywhere, anywhere],
+        out_specs=in_vmem,
+        scratch_shapes=[
+            vmem(value_up.shape, bf16),
+            vmem(w_out.shape, bf16),
+            vmem(w_gate.shape, bf16),
+            vmem(w_up.shape, bf16),
+            vmem(w_down.shape, bf16),
+            vmem(lat.shape, bf16),
+            vmem((512, 512), bf16),
+            vmem((8, 64, w_out.shape[0]), bf16),
+            vmem((16, 32, cols), bf16),
+            vmem((16, 32, cols), bf16),
+            vmem((32, cols), f32),
+            vmem((16, 32, cols), bf16),
+            vmem((2, 64, 2 * ff + 128), f32),
+            vmem((4, 64, 2 * ff + 128), f32),
+            vmem((4, 64, 2 * ff + 128), bf16),
+            vmem((4, 64, 2 * ff + 128), bf16),
+            vmem((4, 64, 2 * ff + 128), bf16),
+            vmem((4, 64, 2 * ff + 128), bf16),
+            vmem((8, 64, ff), bf16),
+            sems((5,)),
+            sems((16,)),
+            sems((16,)),
+            sems((8,)),
+            sems((8,)),
+            sems((16,)),
+            sems((16,)),
+            sems((16,)),
+            sems((16,)),
+            sems((4,)),
+            sems((4,)),
+            sems((4,)),
+            sems((4,)),
+            sems((8,)),
+            sems((8,)),
+            sems((16,)),
+            sems((16,)),
+            sems((16,)),
+            sems((16,)),
+        ],
+        compiler_params=pltpu.CompilerParams(collective_id=1, has_side_effects=True, vmem_limit_bytes=52 * 2**20),
+    )(lat, value_up, hidden.reshape(steps, 8, 32, cols), gain, w_out, w_gate, w_up, w_down)
+    return result.reshape(steps, total, cols)
 
 
 def shards(
@@ -216,34 +533,24 @@
         kv_cache,
         jnp.zeros((), jnp.bfloat16),
     )
-    gain = norm_gain.astype(jnp.float32)
-    results = []
-    for step_no in range(step_count):
-        latent_vectors = jnp.stack(
-            [
-                attend_blocks(
-                    queries[step_no, item], kv_cache[item], my_lengths[item] + step_no, kv_rank
-                )
-                for item in range(req_dev)
-            ]
-        )
-        spread_rows = lax.all_to_all(latent_vectors, "tp", split_axis=1, concat_axis=0, tiled=True)
-        expanded_values = jnp.einsum(
-            "fty,typ->ftp", spread_rows, value_up_weight, preferred_element_type=jnp.float32
-        )
-        expanded_values = expanded_values.astype(jnp.bfloat16).reshape(group_req, -1)
-        head_terms = jnp.dot(
-            lax.all_gather(expanded_values, "dp", axis=0, tiled=True),
-            w_out,
-            preferred_element_type=jnp.float32,
-        )
-        residual = hidden[step_no].astype(jnp.float32)
-        after_attn = residual + tp_whole(head_terms)
-        normed = normalize(after_attn, gain)
-        ffn_out = tp_whole(feed_forward(normed, w_gate, w_up, w_down))
-        layer_row_block = (after_attn + ffn_out).astype(jnp.bfloat16)
-        results.append(layer_row_block)
-    return (new_cache, jnp.stack(results))
+    latents = jnp.stack(
+        [
+            jnp.stack(
+                [
+                    attend_blocks(
+                        queries[step_no, item], kv_cache[item], my_lengths[item] + step_no, kv_rank
+                    )
+                    for step_no in range(step_count)
+                ]
+            )
+            for item in range(req_dev)
+        ]
+    )
+    latents = latents.reshape(req_dev, step_count, tp_count, -1, kv_rank).transpose(2, 0, 1, 3, 4)
+    latents = latents.reshape(tp_count, -1, kv_rank)
+    gain = norm_gain.astype(jnp.float32)[None, :]
+    layer_out = dense(latents, value_up_weight, hidden, gain, w_out, w_gate, w_up, w_down)
+    return (new_cache, layer_out)
 
 
 def solution(mesh):

time: 495 us -> 276 us (0.56)
  waiting for transfers between devices: 238 us -> 0 us
  Pallas kernels: 113 us -> 221 us
  blocking collectives: 42.2 us -> 0 us
  matrix products: 34.2 us -> 18.3 us
  between operations: 15.3 us -> 2.16 us
  starting transfers between devices: 12.4 us -> 0 us
    psum x3 -> x0, waiting for transfers between devices: 238 us -> none  [the longest x2 167 us: tp_whole(): return lax.psum(terms, 'tp')]
    pallas_call x0 -> x1, Pallas kernels: none -> 109 us  [dense(): pl.pallas_call(dense_kernel, out_shape=jax.ShapeDtypeStruct((steps, 8, 32...]
    all_gather x2 -> x0, blocking collectives: 28.4 us -> none  [shards(): lax.all_gather(expanded_values, 'dp', axis=0, tiled=True)]
    dot_general x10 -> x0, matrix products: 20.9 us -> none  [the longest x2 5.99 us: feed_forward(): return jnp.dot(hidden_act, w_down, preferred_element_type=jnp.float32)]
    psum x1 -> x0, blocking collectives: 13.8 us -> none  [normalize(): squares = lax.psum(jnp.sum(rows_in * rows_in, axis=1), 'dp')]
    all_to_all x2 -> x0, starting transfers between devices: 12.1 us -> none  [shards(): lax.all_to_all(latent_vectors, 'tp', split_axis=1, concat_axis=0, tiled=T...]
    dot_general x4, matrix products: 10.4 us -> 15.5 us  [attend_blocks(): jnp.einsum('hc,pc->hp', query_row, key_rows, preferred_element_type=jnp.f...]
    unnamed x35 -> x14, local copies, waits for them, and re-layouts: 10.8 us -> 11.1 us
  transfers between devices with their start and end apart: 5 -> 0, of which waited for: 3 -> 0; matrix products, arithmetic and copies ran while one was open for 5% -> 0% of each run, Pallas kernels for 0% -> 0%
where the time goes in v2:
time: 276 us; the launch traced here: 275 us
  Pallas kernels  221 us (80%)
  local copies, waits for them, and re-layouts  18.7 us (7%)
  matrix products  18.3 us (7%)
  other arithmetic  14.7 us (5%)
    pallas_call x1, Pallas kernels, move(): pl.pallas_call(functools.partial(move_kernel, n_dp, n_tp, chunks), out_sh...  113 us
    pallas_call x1, Pallas kernels, dense(): pl.pallas_call(dense_kernel, out_shape=jax.ShapeDtypeStruct((steps, 8, 32...  109 us
    dot_general x4, matrix products, attend_blocks(): jnp.einsum('hc,pc->hp', query_row, key_rows, preferred_element_type=jnp.f...  15.5 us
    unnamed x14, local copies, waits for them, and re-layouts  11.1 us
    select_n x1, other arithmetic, shards(): jnp.where(positions[None, :, None] < (my_lengths + step_count)[:, None, N...  9.79 us
    squeeze x1, local copies, waits for them, and re-layouts, shards(): kv_cache[item]  5.65 us

profile of v2, /device:TPU:1, one launch (start us, length us, event | category | flops | bytes accessed | tf_op | source)
XLA Modules:
  0.0 275.4 jit_solution(4267255806580877335)
XLA Ops:
  0.6 0.0 copy-start
  0.6 0.8 select_reduce_fusion
  1.5 0.6 gather_fusion
  2.1 0.0 copy-done
  2.1 0.6 gather_fusion.1
  2.8 0.1 iota_compare_fusion.1
  2.9 0.7 fusion.57
  3.6 0.1 dynamic_slice.3
  3.7 0.1 select_reduce_fusion.1.picked
  3.8 0.0 copy-start.3
  3.8 112.7 %shard_map.131 = bf16[2,3072,576]{2,1,0:T(8,128)(2,1)} custom-call(s32[32]{0:T(128)S(1)} %select_reduce_fusion.1.picked, bf16[32,192,576]{2,1,0:T(8,128)(2,1)} %cache.1), custom_call_target="tpu_custom_call" | custom-call | tf_op jit(solution)/shard_map/pallas_call | solution.py:108
  116.6 0.0 copy-done.3
  116.6 0.1 iota_compare_fusion.2
  116.7 9.8 %broadcast_select_fusion = (bf16[2,3072,576]{2,1,0:T(8,128)(2,1)}, bf16[2,3072,576]{2,1,0:T(8,128)(2,1)}) fusion(pred[2,3072]{1,0:T(4,128)(4,1)S(1)} %get-tuple-element.28, bf16[2,3072,576]{2,1,0:T(8,128)(2,1)} %shard_map.131, bf16[2,576]{1,0:T(2,128)(2,1)S(1)} %get-tuple-element.16, pred[2,3072]{1,0:T(4,128)(4,1)S(1)} %get-tuple-element.27, ...), kind=kLoop, calls=%fused_computation.3 | loop fusion | flops 10616832 | bytes 21256704 | tf_op jit(solution)/shard_map/jit(_where)/select_n | solution.py:531
  126.5 10.1 %copy.28 = bf16[2,3072,576]{1,2,0:T(8,128)(2,1)} copy(bf16[2,3072,576]{2,1,0:T(8,128)(2,1)} %get-tuple-element.9) | data formatting | bytes 14155776
  136.6 0.0 copy-start.5
  136.6 5.6 %slice_bitcast_fusion.1 = (bf16[3072,576]{1,0:T(8,128)(2,1)}, bf16[3072,576]{1,0:T(8,128)(2,1)}) fusion(bf16[2,3072,576]{2,1,0:T(8,128)(2,1)} %get-tuple-element.10), kind=kLoop, calls=%fused_computation.5 | loop fusion | bytes 14155776 | tf_op jit(solution)/shard_map/squeeze | solution.py:541
  142.2 0.6 fusion.59
  143.5 0.0 copy-done.5
  143.5 0.0 copy-start.2
  143.5 3.9 %fusion.60 = (f32[128]{0:T(128)S(1)}, f32[3072,128]{1,0:T(8,128)S(1)}) fusion(bf16[2,2,128,576]{2,3,1,0:T(8,128)(2,1)S(1)} %copy-done.5, bf16[2,3072,576]{2,1,0:T(8,128)(2,1)} %get-tuple-element.10, pred[3072]{0:T(1024)(128)(4,1)S(1)} %iota_compare_fusion.5), kind=kOutput, calls=%fused_computation.93 | convolution fusion | flops 454164352 | bytes 5656064 | tf_op jit(solution)/shard_map/hc,pc->hp/dot_general | solution.py:135
  147.5 0.4 fusion.15
  147.9 0.0 copy-done.2
  147.9 0.7 fusion.28
  148.6 0.6 iota_compare_fusion.6
  149.3 3.8 %fusion.61 = (f32[128]{0:T(128)S(1)}, f32[3072,128]{1,0:T(8,128)S(1)}) fusion(bf16[2,2,128,576]{2,3,1,0:T(8,128)(2,1)S(1)} %copy-done.5, bf16[2,3072,576]{2,1,0:T(8,128)(2,1)} %get-tuple-element.10, pred[3072]{0:T(1024)(128)(4,1)S(1)} %iota_compare_fusion.6), kind=kOutput, calls=%fused_computation.94 | convolution fusion | flops 454164352 | bytes 5656064 | tf_op jit(solution)/shard_map/hc,pc->hp/dot_general | solution.py:135
  153.1 0.4 fusion.14
  153.5 0.7 fusion.31
  154.9 0.0 copy-start.1
  154.9 3.9 %fusion.62 = (f32[128]{0:T(128)S(1)}, f32[3072,128]{1,0:T(8,128)S(1)}) fusion(bf16[2,2,128,576]{2,3,1,0:T(8,128)(2,1)S(1)} %copy-done.5, bf16[2,3072,576]{2,1,0:T(8,128)(2,1)} %get-tuple-element.10, pred[3072]{0:T(1024)(128)(4,1)S(1)} %iota_compare_fusion.7), kind=kOutput, calls=%fused_computation.95 | convolution fusion | flops 454164352 | bytes 5656064 | tf_op jit(solution)/shard_map/hc,pc->hp/dot_general | solution.py:135
  158.9 0.4 fusion.13
  159.3 0.0 copy-done.1
  159.3 0.7 fusion.34
  160.0 0.7 iota_compare_fusion.8
  160.7 3.8 %fusion.63 = (f32[128]{0:T(128)S(1)}, f32[3072,128]{1,0:T(8,128)S(1)}) fusion(bf16[2,2,128,576]{2,3,1,0:T(8,128)(2,1)S(1)} %copy-done.5, bf16[2,3072,576]{2,1,0:T(8,128)(2,1)} %get-tuple-element.10, pred[3072]{0:T(1024)(128)(4,1)S(1)} %iota_compare_fusion.8), kind=kOutput, calls=%fused_computation.96 | convolution fusion | flops 454164352 | bytes 5656064 | tf_op jit(solution)/shard_map/hc,pc->hp/dot_general | solution.py:135
  164.5 0.4 fusion.12
  164.9 0.0 copy-start.4
  164.9 0.7 fusion.37
  165.6 0.1 maximum_maximum_fusion
  165.7 0.0 copy-done.4
  165.7 108.8 %shard_map.132 = bf16[2,8,32,896]{3,2,1,0:T(8,128)(2,1)S(1)} custom-call(bf16[16,32,512]{2,1,0:T(8,128)(2,1)S(1)} %bitcast.64, bf16[8,512,128]{2,1,0:T(8,128)(2,1)} %value_up.1, bf16[2,8,32,896]{3,2,1,0:T(8,128)(2,1)} %bitcast.65, f32[1,896]{1,0:T(1,128)S(1)} %reshape.140.gain, bf16[1024,896]{1,0:T(8,128)(2,1)} %w_out.1, bf16[896,1152]{1,0:T(8,128)(2,1)} %w_gate.1, ...), custom_call_target="tpu_custom_call" | custom-call | tf_op jit(solution)/shard_map/pallas_call | solution.py:432
  274.5 0.9 copy.30
  (10 shorter events, 0.1 us)
Async XLA Ops:
  0.6 1.5 copy-start
  3.8 112.8 %copy-start.3 = (bf16[2,2,576]{2,1,0:T(2,128)(2,1)S(1)}, bf16[2,2,576]{2,1,0:T(2,128)(2,1)}, u32[]{:S(2)}) copy-start(bf16[2,2,576]{2,1,0:T(2,128)(2,1)} %param.18) | copy-start | bytes 13828
  136.6 6.9 %copy-start.5 = (bf16[2,2,128,576]{2,3,1,0:T(8,128)(2,1)S(1)}, bf16[2,2,128,576]{2,3,1,0:T(8,128)(2,1)}, u32[]{:S(2)}) copy-start(bf16[2,2,128,576]{2,3,1,0:T(8,128)(2,1)} %param.17) | copy-start | bytes 1769476
  143.5 4.4 %copy-start.2 = (bf16[3072,576]{1,0:T(8,128)(2,1)S(1)}, bf16[3072,576]{1,0:T(8,128)(2,1)}, u32[]{:S(2)}) copy-start(bf16[3072,576]{1,0:T(8,128)(2,1)} %get-tuple-element.14) | copy-start | bytes 10616836
  154.9 4.4 %copy-start.1 = (bf16[3072,576]{1,0:T(8,128)(2,1)S(1)}, bf16[3072,576]{1,0:T(8,128)(2,1)}, u32[]{:S(2)}) copy-start(bf16[3072,576]{1,0:T(8,128)(2,1)} %get-tuple-element.13) | copy-start | bytes 10616836
  164.9 0.8 copy-start.4

commit v3 on v2

--- a/solution.py
+++ b/solution.py
@@ -129,21 +129,72 @@
 norm_eps = 1e-06
 
 
-def attend_blocks(query_row, key_rows, last_pos, kv_rank):
-    context = key_rows.shape[0]
-    raw_all = (
-        jnp.einsum("hc,pc->hp", query_row, key_rows, preferred_element_type=jnp.float32)
-        * score_scale
-    )
-    offsets = jnp.arange(context, dtype=jnp.int32)
-    masked = jnp.where(offsets[None, :] <= last_pos, raw_all, -jnp.inf)
-    row_max = jnp.max(masked, axis=1, keepdims=True)
-    exponent = jnp.exp(masked - row_max)
-    row_total = jnp.sum(exponent, axis=1, keepdims=True)
-    weights = (exponent / row_total).astype(jnp.bfloat16)
-    accum = jnp.dot(weights, key_rows[:, :kv_rank], preferred_element_type=jnp.float32)
-    return accum.astype(jnp.bfloat16)
-
+def attend_kernel(lens, arrived, queries, new_latent, cache_out, lat, scores):
+    f32, bf16 = jnp.float32, jnp.bfloat16
+    item = pl.program_id(0)
+    length = lens[item]
+    context, width = arrived.shape[1:]
+    heads = queries.shape[3]
+    both = 2 * heads
+    kv_rank = lat.shape[2]
+    query = jnp.concatenate([queries[0, 0], queries[1, 0]], axis=1)
+    first = new_latent[0, item].astype(f32)
+    second = new_latent[1, item].astype(f32)
+    block = 256
+    row = lax.broadcasted_iota(jnp.int32, (block, width), 0)
+    place = lax.broadcasted_iota(jnp.int32, (block, both), 0)
+    last = length + lax.broadcasted_iota(jnp.int32, (block, both), 1) // heads
+
+    def score(i, top):
+        start = pl.multiple_of(i * block, block)
+        rows = pl.ds(start, block)
+        position = row + start
+        keys = arrived[0, rows].astype(f32)
+        keys = jnp.where(position < length, keys, jnp.where(position == length, first, jnp.where(position == length + 1, second, 0.0)))
+        keys = keys.astype(bf16)
+        cache_out[0, :, rows] = keys.T
+        raw = jnp.dot(keys, query, preferred_element_type=f32) * score_scale
+        raw = jnp.where(place + start <= last, raw, -jnp.inf)
+        scores[rows] = raw
+        return jnp.maximum(top, jnp.max(raw, axis=0, keepdims=True))
+
+    top = lax.fori_loop(0, context // block, score, jnp.full((1, both), -jnp.inf, f32))
+    exponent = jnp.exp(scores[...] - top)
+    total = jnp.sum(exponent, axis=0, keepdims=True)
+    mixed_t = jnp.dot(cache_out[0, :kv_rank], exponent.astype(bf16), preferred_element_type=f32)
+    mixed = (mixed_t / total).T
+    mixed = mixed.reshape(2, lat.shape[0], -1, kv_rank)
+    mixed = jnp.concatenate([mixed[0], mixed[1]], axis=1).astype(bf16)
+    lat[:, pl.ds(pl.multiple_of(item * 16, 16), 16)] = mixed
+
+
+def attend(my_lengths, arrived, queries, new_latent, n_tp, kv_rank):
+    items, context, width = arrived.shape
+    steps, _, heads, _ = queries.shape
+    bf16 = jnp.bfloat16
+    flipped, latents = pl.pallas_call(
+        attend_kernel,
+        grid=(items,),
+        out_shape=(
+            jax.ShapeDtypeStruct((items, width, context), bf16),
+            jax.ShapeDtypeStruct((n_tp, items * steps * heads // n_tp, kv_rank), bf16),
+        ),
+        in_specs=[
+            pl.BlockSpec(memory_space=pltpu.SMEM),
+            pl.BlockSpec((1, context, width), lambda i: (i, 0, 0)),
+            pl.BlockSpec((steps, 1, width, heads), lambda i: (0, i, 0, 0)),
+            pl.BlockSpec((steps, items, 1, width), lambda i: (0, 0, 0, 0)),
+        ],
+        out_specs=(
+            pl.BlockSpec((1, width, context), lambda i: (i, 0, 0)),
+            pl.BlockSpec((n_tp, items * steps * heads // n_tp, kv_rank), lambda i: (0, 0, 0)),
+        ),
+        scratch_shapes=[
+            pltpu.VMEM((context, steps * heads), jnp.float32),
+        ],
+        compiler_params=pltpu.CompilerParams(vmem_limit_bytes=40 * 2**20),
+    )(my_lengths, arrived, queries.transpose(0, 1, 3, 2), new_latent[:, :, None, :])
+    return flipped.transpose(0, 2, 1), latents
 
 def dense_kernel(
     lat,
@@ -497,12 +548,10 @@
     tp_count = lax.axis_size("tp")
     my_group = lax.axis_index("dp")
     my_column = lax.axis_index("tp")
-    group_req, piece_len, lat_width = old_cache.shape
+    group_req = old_cache.shape[0]
     per_pair = group_req // dp_count
-    step_count = queries.shape[0]
     req_dev = queries.shape[1]
     req_total = new_slot.shape[0]
-    context = piece_len * tp_count
     kv_rank = value_up_weight.shape[1]
     everyone = jnp.arange(req_total, dtype=jnp.int32)
     new_group = new_slot // group_req
@@ -520,34 +569,7 @@
     )
     my_slots = (my_group * tp_count + my_column) * req_dev + jnp.arange(req_dev, dtype=jnp.int32)
     my_lengths = jnp.take(lengths, jnp.take(source, my_slots))
-    positions = jnp.arange(context, dtype=jnp.int32)
-    kv_cache = arrived
-    for step_no in range(step_count):
-        kv_cache = jnp.where(
-            positions[None, :, None] == (my_lengths + step_no)[:, None, None],
-            new_latent[step_no][:, None, :],
-            kv_cache,
-        )
-    new_cache = jnp.where(
-        positions[None, :, None] < (my_lengths + step_count)[:, None, None],
-        kv_cache,
-        jnp.zeros((), jnp.bfloat16),
-    )
-    latents = jnp.stack(
-        [
-            jnp.stack(
-                [
-                    attend_blocks(
-                        queries[step_no, item], kv_cache[item], my_lengths[item] + step_no, kv_rank
-                    )
-                    for step_no in range(step_count)
-                ]
-            )
-            for item in range(req_dev)
-        ]
-    )
-    latents = latents.reshape(req_dev, step_count, tp_count, -1, kv_rank).transpose(2, 0, 1, 3, 4)
-    latents = latents.reshape(tp_count, -1, kv_rank)
+    new_cache, latents = attend(my_lengths, arrived, queries, new_latent, tp_count, kv_rank)
     gain = norm_gain.astype(jnp.float32)[None, :]
     layer_out = dense(latents, value_up_weight, hidden, gain, w_out, w_gate, w_up, w_down)
     return (new_cache, layer_out)

time: 276 us -> 242 us (0.88)
  matrix products: 18.3 us -> 0 us
  local copies, waits for them, and re-layouts: 18.7 us -> 5.54 us
  other arithmetic: 14.7 us -> 1.64 us
  Pallas kernels: 221 us -> 234 us
    dot_general x8 -> x0, matrix products: 18.3 us -> none  [the longest x4 15.5 us: attend_blocks(): jnp.einsum('hc,pc->hp', query_row, key_rows, preferred_element_type=jnp.f...]
    pallas_call x0 -> x1, Pallas kernels: none -> 11.1 us  [attend(): pl.pallas_call(attend_kernel, grid=(items,), out_shape=(jax.ShapeDtypeStr...]
    select_n x1 -> x0, other arithmetic: 9.79 us -> none  [shards(): jnp.where(positions[None, :, None] < (my_lengths + step_count)[:, None, N...]
    unnamed x14 -> x11, local copies, waits for them, and re-layouts: 11.1 us -> 4.17 us
    squeeze x1 -> x0, local copies, waits for them, and re-layouts: 5.65 us -> none  [shards(): kv_cache[item]]
where the time goes in v3:
time: 242 us
  Pallas kernels  234 us (97%)
  local copies, waits for them, and re-layouts  5.54 us (2%)
    pallas_call x1, Pallas kernels, move(): pl.pallas_call(functools.partial(move_kernel, n_dp, n_tp, chunks), out_sh...  113 us
    pallas_call x1, Pallas kernels, dense(): pl.pallas_call(dense_kernel, out_shape=jax.ShapeDtypeStruct((steps, 8, 32...  110 us
    pallas_call x1, Pallas kernels, attend(): pl.pallas_call(attend_kernel, grid=(items,), out_shape=(jax.ShapeDtypeStr...  11.1 us

profile of v3, /device:TPU:1, one launch (start us, length us, event | category | flops | bytes accessed | tf_op | source)
XLA Modules:
  0.0 242.1 jit_solution(9787138040316940273)
XLA Ops:
  0.6 0.0 copy-start
  0.7 0.8 select_reduce_fusion
  1.5 0.6 gather_fusion
  2.1 0.0 copy-done
  2.1 0.6 gather_fusion.1
  2.8 0.7 fusion.1
  3.5 0.1 dynamic_slice.3
  3.6 0.1 select_reduce_fusion.1.picked
  3.7 0.0 copy-start.3
  3.7 0.0 copy-start.2
  3.7 112.7 %shard_map.131.arrived = bf16[2,3072,576]{2,1,0:T(8,128)(2,1)} custom-call(s32[32]{0:T(128)S(1)} %select_reduce_fusion.1.picked, bf16[32,192,576]{2,1,0:T(8,128)(2,1)} %cache.1), custom_call_target="tpu_custom_call" | custom-call | tf_op jit(solution)/shard_map/pallas_call | solution.py:108
  116.5 0.0 copy-done.3
  116.5 0.0 copy-done.2
  116.5 0.0 copy-start.1
  116.5 3.2 %copy-done.1 = bf16[2,3072,576]{2,1,0:T(8,128)(2,1)S(1)} copy-done((bf16[2,3072,576]{2,1,0:T(8,128)(2,1)S(1)}, bf16[2,3072,576]{2,1,0:T(8,128)(2,1)}, u32[]{:S(2)}) %copy-start.1) | copy-done | bytes 7077912
  119.7 0.0 copy-start.4
  119.7 11.1 %shard_map.132 = (bf16[2,576,3072]{2,1,0:T(8,128)(2,1)}, bf16[16,32,512]{2,1,0:T(8,128)(2,1)S(1)}) custom-call(s32[2]{0:T(128)S(1)} %and_select_fusion.lens, bf16[2,3072,576]{2,1,0:T(8,128)(2,1)S(1)} %copy-done.1, bf16[2,2,576,128]{3,2,1,0:T(8,128)(2,1)S(1)} %bitcast.6, bf16[2,2,1,576]{3,2,1,0:T(2,128)(2,1)S(1)} %copy.15.new_latent), custom_call_target="tpu_custom_call" | custom-call | tf_op jit(solution)/shard_map/pallas_call | solution.py:175
  130.8 0.0 copy-done.4
  130.8 110.4 %shard_map.133 = bf16[2,8,32,896]{3,2,1,0:T(8,128)(2,1)S(1)} custom-call(bf16[16,32,512]{2,1,0:T(8,128)(2,1)S(1)} %get-tuple-element.6.lat, bf16[8,512,128]{2,1,0:T(8,128)(2,1)} %value_up.1, bf16[2,8,32,896]{3,2,1,0:T(8,128)(2,1)} %bitcast.7, f32[1,896]{1,0:T(1,128)S(1)} %reshape.19.gain, bf16[1024,896]{1,0:T(8,128)(2,1)} %w_out.1, ...), custom_call_target="tpu_custom_call" | custom-call | tf_op jit(solution)/shard_map/pallas_call | solution.py:483
  241.2 0.9 copy.17
  (7 shorter events, 0.1 us)
Async XLA Ops:
  0.6 1.5 copy-start
  3.7 112.8 %copy-start.3 = (bf16[2,2,576]{2,1,0:T(2,128)(2,1)S(1)}, bf16[2,2,576]{2,1,0:T(2,128)(2,1)}, u32[]{:S(2)}) copy-start(bf16[2,2,576]{2,1,0:T(2,128)(2,1)} %param.18) | copy-start | bytes 13828
  3.7 112.8 %copy-start.2 = (bf16[2,2,128,576]{2,3,1,0:T(8,128)(2,1)S(1)}, bf16[2,2,128,576]{2,3,1,0:T(8,128)(2,1)}, u32[]{:S(2)}) copy-start(bf16[2,2,128,576]{2,3,1,0:T(8,128)(2,1)} %param.17) | copy-start | bytes 1769476
  116.5 3.2 %copy-start.1 = (bf16[2,3072,576]{2,1,0:T(8,128)(2,1)S(1)}, bf16[2,3072,576]{2,1,0:T(8,128)(2,1)}, u32[]{:S(2)}) copy-start(bf16[2,3072,576]{2,1,0:T(8,128)(2,1)} %shard_map.131.arrived) | copy-start | bytes 21233668
  119.7 11.1 %copy-start.4 = (bf16[896]{0:T(1024)(128)(2,1)S(1)}, bf16[896]{0:T(1024)(128)(2,1)}, u32[]{:S(2)}) copy-start(bf16[896]{0:T(1024)(128)(2,1)} %param.22) | copy-start | bytes 5380

commit v4 on v3

--- a/solution.py
+++ b/solution.py
@@ -219,7 +219,6 @@
     after,
     ybuf,
     gu,
-    keep,
     pair_s,
     pair_r,
     ring_s,
@@ -254,10 +253,11 @@
     ff = wgate_v.shape[1]
     width = 2 * ff
 
-    def owner(block):
-        return 4 * lax.rem(block, 4) + lax.rem(lax.rem(block, 4) + block // 4, 4)
-
-    mine = 4 * lax.rem(x - z + 4, 4) + z
+    def block_of(column):
+        down = column // 4
+        return 4 * lax.rem(lax.rem(column, 4) - down + 4, 4) + down
+
+    mine = block_of(c)
 
     loads = []
     for n, (src, dst) in enumerate(
@@ -292,86 +292,80 @@
     loads[0].wait()
     for head in range(8):
         part = jnp.dot(ordered[64 * head : 64 * head + 64], vup_v[head], preferred_element_type=f32)
-        xbuf[g, :, 128 * head : 128 * head + 128] = part.astype(bf16)
-
-    def gather_ring(buf, ss, rs, i, source):
+        xbuf[0, g, :, 128 * head : 128 * head + 128] = part[:32].astype(bf16)
+        xbuf[1, g, :, 128 * head : 128 * head + 128] = part[32:].astype(bf16)
+
+    def gather_ring(buf, ss, rs, s, i, source):
         to = lax.rem(g + 2 * i, 8)
-        return remote(buf.at[g], buf.at[source], ss.at[i], rs.at[source], to, c)
-
-    def gather_pair(buf, ss, rs, i, sent, got):
-        return remote(buf.at[sent], buf.at[got], ss.at[4 + i], rs.at[got], sib, c)
-
-    def gather_start(buf, ss, rs):
-        loop(1, 4, lambda i: gather_ring(buf, ss, rs, i, g).start())
-        gather_pair(buf, ss, rs, 0, g, g).start()
-
-    def gather_step(buf, ss, rs, i):
-        src = lax.rem(g + 8 - 2 * i, 8)
-        other = src + 1 - 2 * k
-
-        @pl.when(i > 0)
-        def _():
-            gather_ring(buf, ss, rs, i, src).wait_recv()
-            gather_pair(buf, ss, rs, i, src, src).start()
-
-        gather_pair(buf, ss, rs, i, src, other).wait_recv()
-        return src // 2
-
-    def gather_end(buf, ss, rs):
-        loop(1, 4, lambda i: gather_ring(buf, ss, rs, i, g).wait_send())
-        loop(0, 4, lambda i: gather_pair(buf, ss, rs, i, g, g).wait_send())
-
-    def scatter_copy(ss, rs, block, source):
-        return remote(s3.at[block], r3.at[source], ss.at[block], rs.at[source], g, owner(block))
-
-    def scatter(value, chunk, ss, rs):
-        for j in range(4):
-            s3[4 * chunk + j] = value[32 * j : 32 * j + 32].astype(bf16)
-        for j in range(4):
-            block = 4 * chunk + j
-
-            @pl.when(block != mine)
-            def _():
-                scatter_copy(ss, rs, block, c).start()
-
-    def scatter_sum(ss, rs, first):
-        total = first
-        loop(1, 16, lambda i: scatter_copy(ss, rs, mine, lax.rem(c + 16 - i, 16)).wait_recv())
-        r3[c] = s3[mine]
-        total = total + jnp.sum(r3[...].astype(f32), axis=0)
-        def sent(i):
-            @pl.when(i != mine)
-            def _():
-                scatter_copy(ss, rs, i, c).wait_send()
-        loop(0, 16, sent)
+        return remote(buf.at[s, g], buf.at[s, source], ss.at[s, i], rs.at[s, source], to, c)
+
+    def gather_pair(buf, ss, rs, s, i, sent, got):
+        return remote(buf.at[s, sent], buf.at[s, got], ss.at[s, 4 + i], rs.at[s, got], sib, c)
+
+    def gather_start(buf, ss, rs, s):
+        loop(1, 4, lambda i: gather_ring(buf, ss, rs, s, i, g).start())
+        gather_pair(buf, ss, rs, s, 0, g, g).start()
+
+    def gather_rest(buf, ss, rs, s):
+        def forward(i):
+            src = lax.rem(g + 8 - 2 * i, 8)
+            gather_ring(buf, ss, rs, s, i, src).wait_recv()
+            gather_pair(buf, ss, rs, s, i, src, src).start()
+
+        loop(1, 4, forward)
+        loop(0, 4, lambda i: gather_pair(buf, ss, rs, s, i, g, lax.rem(sib + 8 - 2 * i, 8)).wait_recv())
+
+    def gather_end(buf, ss, rs, s):
+        loop(1, 4, lambda i: gather_ring(buf, ss, rs, s, i, g).wait_send())
+        loop(0, 4, lambda i: gather_pair(buf, ss, rs, s, i, g, g).wait_send())
+
+    def scatter_copy(ss, rs, s, i, source):
+        to = lax.rem(c + i, 16)
+        return remote(s3.at[s, block_of(to)], r3.at[s, source], ss.at[s, to], rs.at[s, source], g, to)
+
+    def scatter(value, ss, rs, s):
+        s3[s] = value.reshape(16, 16, value.shape[1]).astype(bf16)
+        loop(1, 16, lambda i: scatter_copy(ss, rs, s, i, c).start())
+
+    def scatter_sum(ss, rs, s, first):
+        r3[s, c] = s3[s, mine]
+        loop(1, 16, lambda i: scatter_copy(ss, rs, s, i, lax.rem(c + 16 - i, 16)).wait_recv())
+        total = first + jnp.sum(r3[s].astype(f32), axis=0)
+        loop(1, 16, lambda i: scatter_copy(ss, rs, s, i, c).wait_send())
         return total
 
-    gather_start(xbuf, x_ss, x_rs)
+    def spread(buf, ss, rs, s, i, source):
+        to = lax.rem(c + i, 16)
+        return remote(buf.at[s, mine], buf.at[s, block_of(source)], ss.at[s, to], rs.at[s, source], g, to)
+
+    def spread_start(buf, ss, rs, s):
+        loop(1, 16, lambda i: spread(buf, ss, rs, s, i, c).start())
+
+    def spread_wait(buf, ss, rs, s):
+        loop(1, 16, lambda i: spread(buf, ss, rs, s, i, lax.rem(c + 16 - i, 16)).wait_recv())
+
+    def spread_end(buf, ss, rs, s):
+        loop(1, 16, lambda i: spread(buf, ss, rs, s, i, c).wait_send())
+
+    loop(0, 2, lambda s: gather_start(xbuf, x_ss, x_rs, s))
     loads[1].wait()
 
-    def out_step(i):
-        chunk = gather_step(xbuf, x_ss, x_rs, i)
-        rows = xbuf[pl.ds(2 * chunk, 2)].reshape(128, 1024)
-        scatter(jnp.dot(rows, wout_v[...], preferred_element_type=f32), chunk, s3_ss, s3_rs)
-
-    loop(0, 4, out_step)
-    residual = hidden[lax.rem(mine, 2), mine // 2].astype(f32)
-    after[...] = scatter_sum(s3_ss, s3_rs, residual)
-    gather_end(xbuf, x_ss, x_rs)
-
-    ybuf[mine] = after[...].astype(bf16)
-
-    def spread(buf_at, ss, rs, i, block):
-        to = lax.rem(c + i, 16)
-        return remote(buf_at(mine), buf_at(block), ss.at[to], rs.at[block], g, to)
-
-    def y_at(block):
-        return ybuf.at[block]
-
-    loop(1, 16, lambda i: spread(y_at, y_ss, y_rs, i, mine).start())
+    def out_stage(s):
+        gather_rest(xbuf, x_ss, x_rs, s)
+        rows = xbuf[s].reshape(256, xbuf.shape[3])
+        scatter(jnp.dot(rows, wout_v[...], preferred_element_type=f32), s3_ss, s3_rs, s)
+
+    loop(0, 2, out_stage)
+
+    def after_stage(s):
+        after[s] = scatter_sum(s3_ss, s3_rs, s, hidden[s, mine].astype(f32))
+        ybuf[s, mine] = after[s].astype(bf16)
+        spread_start(ybuf, y_ss, y_rs, s)
+
+    loop(0, 2, after_stage)
     loads[2].wait()
     loads[3].wait()
-    lane = lax.broadcasted_iota(jnp.int32, (64, 128), 1)
+    lane = lax.broadcasted_iota(jnp.int32, (32, 128), 1)
 
     def two_part(total):
         high = total.astype(bf16)
@@ -381,97 +375,90 @@
     def one_part(pair):
         return pair[:, 0:1].astype(f32) + pair[:, 64:65].astype(f32)
 
-    def pair_copy(chunk):
-        return remote(pair_s.at[chunk], pair_r.at[chunk], pair_ss.at[chunk], pair_rs.at[chunk], sib, c)
-
-    def ring_copy(chunk, source):
-        return remote(ring_s.at[chunk], ring_r.at[source], ring_ss.at[chunk], ring_rs.at[source], 2 * chunk + k, c)
-
-    def gate_step(i):
-        chunk = lax.rem(y + 1 + i, 4)
-        for j in range(4):
-            block = 4 * chunk + j
-
-            @pl.when(block != mine)
-            def _():
-                spread(y_at, y_ss, y_rs, 1, block).wait_recv()
-
-        rows = ybuf[pl.ds(4 * chunk, 4)].reshape(128, ybuf.shape[2]).astype(f32)
+    def pair_copy(s, chunk):
+        return remote(pair_s.at[s, chunk], pair_r.at[s, chunk], pair_ss.at[s, chunk], pair_rs.at[s, chunk], sib, c)
+
+    def ring_copy(s, chunk, source):
+        return remote(
+            ring_s.at[s, chunk], ring_r.at[s, source], ring_ss.at[s, chunk], ring_rs.at[s, source], 2 * chunk + k, c
+        )
+
+    def gate_stage(s):
+        spread_wait(ybuf, y_ss, y_rs, s)
+        rows = ybuf[s].reshape(256, ybuf.shape[3]).astype(f32)
         squares = jnp.sum(rows * rows, axis=1, keepdims=True)
         scaled = (rows * gain[...]).astype(bf16)
-        gu[:, :, 0:ff] = jnp.dot(scaled, wgate_v[...], preferred_element_type=f32).reshape(2, 64, ff)
-        gu[:, :, ff:width] = jnp.dot(scaled, wup_v[...], preferred_element_type=f32).reshape(2, 64, ff)
-        gu[:, :, width : width + 128] = jnp.broadcast_to(squares, (128, 128)).reshape(2, 64, 128)
-        pair_s[chunk, :, 0:width] = gu[1 - k, :, 0:width].astype(bf16)
-        pair_s[chunk, :, width : width + 128] = two_part(gu[1 - k, :, width : width + 128])
-        pair_copy(chunk).start()
-        keep[chunk] = gu[k]
-
-    def merge_step(i):
-        chunk = lax.rem(y + 1 + i, 4)
-        pair_copy(chunk).wait_recv()
-        keep[chunk, :, 0:width] += pair_r[chunk, :, 0:width].astype(f32)
-        keep[chunk, :, width : width + 128] += one_part(pair_r[chunk, :, width : width + 128])
-
-        @pl.when(chunk != y)
-        def _():
-            ring_s[chunk, :, 0:width] = keep[chunk, :, 0:width].astype(bf16)
-            ring_s[chunk, :, width : width + 128] = two_part(keep[chunk, :, width : width + 128])
-            ring_copy(chunk, y).start()
-
-    def gate_loop(i):
-        @pl.when(i < 4)
-        def _():
-            gate_step(i)
-
-        @pl.when(i > 0)
-        def _():
-            merge_step(i - 1)
-
-    loop(0, 5, gate_loop)
-
-    def ring_add(i):
-        source = lax.rem(y + i, 4)
-        ring_copy(source, source).wait_recv()
-        keep[y, :, 0:width] += ring_r[source, :, 0:width].astype(f32)
-        keep[y, :, width : width + 128] += one_part(ring_r[source, :, width : width + 128])
-
-    loop(1, 4, ring_add)
-    squares = keep[y, :, width : width + 1]
-    scale = 1.0 / jnp.sqrt(squares / D + norm_eps)
-    gate = keep[y, :, 0:ff] * scale
-    up = keep[y, :, ff:width] * scale
-    hbuf[g] = (jax.nn.silu(gate) * up).astype(bf16)
-    gather_start(hbuf, h_ss, h_rs)
+        gu[s, :, :, :, width : width + 128] = jnp.broadcast_to(squares, (256, 128)).reshape(4, 2, 32, 128)
+        gu[s, :, :, :, 0:ff] = jnp.dot(scaled, wgate_v[...], preferred_element_type=f32).reshape(4, 2, 32, ff)
+        gu[s, :, :, :, ff:width] = jnp.dot(scaled, wup_v[...], preferred_element_type=f32).reshape(4, 2, 32, ff)
+
+        def give(i):
+            chunk = lax.rem(y + 1 + i, 4)
+            pair_s[s, chunk, :, 0:width] = gu[s, chunk, 1 - k, :, 0:width].astype(bf16)
+            pair_s[s, chunk, :, width : width + 128] = two_part(gu[s, chunk, 1 - k, :, width : width + 128])
+            pair_copy(s, chunk).start()
+
+        loop(0, 4, give)
+
+        def merge(i):
+            chunk = lax.rem(y + 1 + i, 4)
+            pair_copy(s, chunk).wait_recv()
+            total = gu[s, chunk, k, :, 0:width] + pair_r[s, chunk, :, 0:width].astype(f32)
+            squares = gu[s, chunk, k, :, width : width + 128] + one_part(pair_r[s, chunk, :, width : width + 128])
+            gu[s, chunk, k, :, 0:width] = total
+            gu[s, chunk, k, :, width : width + 128] = squares
+
+            @pl.when(chunk != y)
+            def _():
+                ring_s[s, chunk, :, 0:width] = total.astype(bf16)
+                ring_s[s, chunk, :, width : width + 128] = two_part(squares)
+                ring_copy(s, chunk, y).start()
+
+        loop(0, 4, merge)
+
+    loop(0, 2, gate_stage)
+
+    def act_stage(s):
+        def ring_add(i):
+            source = lax.rem(y + i, 4)
+            ring_copy(s, source, source).wait_recv()
+            gu[s, y, k, :, 0:width] += ring_r[s, source, :, 0:width].astype(f32)
+            gu[s, y, k, :, width : width + 128] += one_part(ring_r[s, source, :, width : width + 128])
+
+        loop(1, 4, ring_add)
+        scale = 1.0 / jnp.sqrt(gu[s, y, k, :, width : width + 1] / D + norm_eps)
+        gate = gu[s, y, k, :, 0:ff] * scale
+        up = gu[s, y, k, :, ff:width] * scale
+        hbuf[s, g] = (jax.nn.silu(gate) * up).astype(bf16)
+        gather_start(hbuf, h_ss, h_rs, s)
+
+    loop(0, 2, act_stage)
     loads[4].wait()
 
-    def down_step(i):
-        chunk = gather_step(hbuf, h_ss, h_rs, i)
-        rows = hbuf[pl.ds(2 * chunk, 2)].reshape(128, ff)
-        scatter(jnp.dot(rows, wdown_v[...], preferred_element_type=f32), chunk, s7_ss, s7_rs)
-
-    loop(0, 4, down_step)
-    result = scatter_sum(s7_ss, s7_rs, after[...])
-    step, group = lax.rem(mine, 2), mine // 2
-    out[step, group] = result.astype(bf16)
-
-    def o_at(block):
-        return out.at[lax.rem(block, 2), block // 2]
-
-    loop(1, 16, lambda i: spread(o_at, o_ss, o_rs, i, mine).start())
-    gather_end(hbuf, h_ss, h_rs)
+    def down_stage(s):
+        gather_rest(hbuf, h_ss, h_rs, s)
+        rows = hbuf[s].reshape(256, ff)
+        scatter(jnp.dot(rows, wdown_v[...], preferred_element_type=f32), s7_ss, s7_rs, s)
+
+    loop(0, 2, down_stage)
+
+    def result_stage(s):
+        out[s, mine] = scatter_sum(s7_ss, s7_rs, s, after[s]).astype(bf16)
+        spread_start(out, o_ss, o_rs, s)
+
+    loop(0, 2, result_stage)
     loop(1, 16, lambda i: lat_copy(i, c).wait_send())
-    loop(1, 16, lambda i: spread(y_at, y_ss, y_rs, i, mine).wait_send())
-    loop(0, 4, lambda i: pair_copy(i).wait_send())
-    loop(1, 4, lambda i: ring_copy(lax.rem(y + i, 4), y).wait_send())
-
-    def finish(block):
-        @pl.when(block != mine)
-        def _():
-            spread(o_at, o_ss, o_rs, 1, block).wait_recv()
-
-    loop(0, 16, finish)
-    loop(1, 16, lambda i: spread(o_at, o_ss, o_rs, i, mine).wait_send())
+
+    def end_stage(s):
+        gather_end(xbuf, x_ss, x_rs, s)
+        spread_end(ybuf, y_ss, y_rs, s)
+        loop(0, 4, lambda i: pair_copy(s, i).wait_send())
+        loop(1, 4, lambda i: ring_copy(s, lax.rem(y + i, 4), y).wait_send())
+        gather_end(hbuf, h_ss, h_rs, s)
+        spread_end(out, o_ss, o_rs, s)
+        spread_wait(out, o_ss, o_rs, s)
+
+    loop(0, 2, end_stage)
 
 
 def dense(lat, value_up, hidden, gain, w_out, w_gate, w_up, w_down):
@@ -482,7 +469,7 @@
     in_vmem, anywhere = pl.BlockSpec(memory_space=pltpu.VMEM), pl.BlockSpec(memory_space=pl.ANY)
     result = pl.pallas_call(
         dense_kernel,
-        out_shape=jax.ShapeDtypeStruct((steps, 8, 32, cols), bf16),
+        out_shape=jax.ShapeDtypeStruct((steps, 16, 16, cols), bf16),
         in_specs=[in_vmem, anywhere, in_vmem, in_vmem, anywhere, anywhere, anywhere, anywhere],
         out_specs=in_vmem,
         scratch_shapes=[
@@ -493,40 +480,39 @@
             vmem(w_down.shape, bf16),
             vmem(lat.shape, bf16),
             vmem((512, 512), bf16),
-            vmem((8, 64, w_out.shape[0]), bf16),
-            vmem((16, 32, cols), bf16),
-            vmem((16, 32, cols), bf16),
-            vmem((32, cols), f32),
-            vmem((16, 32, cols), bf16),
-            vmem((2, 64, 2 * ff + 128), f32),
-            vmem((4, 64, 2 * ff + 128), f32),
-            vmem((4, 64, 2 * ff + 128), bf16),
-            vmem((4, 64, 2 * ff + 128), bf16),
-            vmem((4, 64, 2 * ff + 128), bf16),
-            vmem((4, 64, 2 * ff + 128), bf16),
-            vmem((8, 64, ff), bf16),
+            vmem((2, 8, 32, w_out.shape[0]), bf16),
+            vmem((2, 16, 16, cols), bf16),
+            vmem((2, 16, 16, cols), bf16),
+            vmem((2, 16, cols), f32),
+            vmem((2, 16, 16, cols), bf16),
+            vmem((2, 4, 2, 32, 2 * ff + 128), f32),
+            vmem((2, 4, 32, 2 * ff + 128), bf16),
+            vmem((2, 4, 32, 2 * ff + 128), bf16),
+            vmem((2, 4, 32, 2 * ff + 128), bf16),
+            vmem((2, 4, 32, 2 * ff + 128), bf16),
+            vmem((2, 8, 32, ff), bf16),
             sems((5,)),
             sems((16,)),
             sems((16,)),
-            sems((8,)),
-            sems((8,)),
-            sems((16,)),
-            sems((16,)),
-            sems((16,)),
-            sems((16,)),
-            sems((4,)),
-            sems((4,)),
-            sems((4,)),
-            sems((4,)),
-            sems((8,)),
-            sems((8,)),
-            sems((16,)),
-            sems((16,)),
-            sems((16,)),
-            sems((16,)),
+            sems((2, 8)),
+            sems((2, 8)),
+            sems((2, 16)),
+            sems((2, 16)),
+            sems((2, 16)),
+            sems((2, 16)),
+            sems((2, 4)),
+            sems((2, 4)),
+            sems((2, 4)),
+            sems((2, 4)),
+            sems((2, 8)),
+            sems((2, 8)),
+            sems((2, 16)),
+            sems((2, 16)),
+            sems((2, 16)),
+            sems((2, 16)),
         ],
         compiler_params=pltpu.CompilerParams(collective_id=1, has_side_effects=True, vmem_limit_bytes=52 * 2**20),
-    )(lat, value_up, hidden.reshape(steps, 8, 32, cols), gain, w_out, w_gate, w_up, w_down)
+    )(lat, value_up, hidden.reshape(steps, 16, 16, cols), gain, w_out, w_gate, w_up, w_down)
     return result.reshape(steps, total, cols)
 
 

time: 242 us -> 224 us (0.926)
  Pallas kernels: 234 us -> 216 us
    pallas_call x1, Pallas kernels: 110 us -> 91.8 us  [dense(): pl.pallas_call(dense_kernel, out_shape=jax.ShapeDtypeStruct((steps, 16, 1...]
where the time goes in v4:
time: 224 us
  Pallas kernels  216 us (96%)
  local copies, waits for them, and re-layouts  5.54 us (2%)
    pallas_call x1, Pallas kernels, move(): pl.pallas_call(functools.partial(move_kernel, n_dp, n_tp, chunks), out_sh...  113 us
    pallas_call x1, Pallas kernels, dense(): pl.pallas_call(dense_kernel, out_shape=jax.ShapeDtypeStruct((steps, 16, 1...  91.8 us
    pallas_call x1, Pallas kernels, attend(): pl.pallas_call(attend_kernel, grid=(items,), out_shape=(jax.ShapeDtypeStr...  11.1 us

profile of v4, /device:TPU:1, one launch (start us, length us, event | category | flops | bytes accessed | tf_op | source)
XLA Modules:
  0.0 223.5 jit_solution(10916057655622284875)
XLA Ops:
  0.6 0.0 copy-start
  0.7 0.8 select_reduce_fusion
  1.5 0.6 gather_fusion
  2.1 0.0 copy-done
  2.1 0.6 gather_fusion.1
  2.8 0.7 fusion.1
  3.5 0.1 dynamic_slice.3
  3.6 0.1 select_reduce_fusion.1.picked
  3.7 0.0 copy-start.3
  3.7 0.0 copy-start.2
  3.7 112.7 %shard_map.131.arrived = bf16[2,3072,576]{2,1,0:T(8,128)(2,1)} custom-call(s32[32]{0:T(128)S(1)} %select_reduce_fusion.1.picked, bf16[32,192,576]{2,1,0:T(8,128)(2,1)} %cache.1), custom_call_target="tpu_custom_call" | custom-call | tf_op jit(solution)/shard_map/pallas_call | solution.py:108
  116.5 0.0 copy-done.3
  116.5 0.0 copy-done.2
  116.5 0.0 copy-start.1
  116.5 3.2 %copy-done.1 = bf16[2,3072,576]{2,1,0:T(8,128)(2,1)S(1)} copy-done((bf16[2,3072,576]{2,1,0:T(8,128)(2,1)S(1)}, bf16[2,3072,576]{2,1,0:T(8,128)(2,1)}, u32[]{:S(2)}) %copy-start.1) | copy-done | bytes 7077912
  119.7 0.0 copy-start.4
  119.7 11.1 %shard_map.132 = (bf16[2,576,3072]{2,1,0:T(8,128)(2,1)}, bf16[16,32,512]{2,1,0:T(8,128)(2,1)S(1)}) custom-call(s32[2]{0:T(128)S(1)} %and_select_fusion.lens, bf16[2,3072,576]{2,1,0:T(8,128)(2,1)S(1)} %copy-done.1, bf16[2,2,576,128]{3,2,1,0:T(8,128)(2,1)S(1)} %bitcast.6, bf16[2,2,1,576]{3,2,1,0:T(2,128)(2,1)S(1)} %copy.15.new_latent), custom_call_target="tpu_custom_call" | custom-call | tf_op jit(solution)/shard_map/pallas_call | solution.py:175
  130.8 0.0 copy-done.4
  130.8 91.8 %shard_map.133 = bf16[2,16,16,896]{3,2,1,0:T(8,128)(2,1)S(1)} custom-call(bf16[16,32,512]{2,1,0:T(8,128)(2,1)S(1)} %get-tuple-element.6.lat, bf16[8,512,128]{2,1,0:T(8,128)(2,1)} %value_up.1, bf16[2,16,16,896]{3,2,1,0:T(8,128)(2,1)} %bitcast.7, f32[1,896]{1,0:T(1,128)S(1)} %reshape.19.gain, bf16[1024,896]{1,0:T(8,128)(2,1)} %w_out.1, ...), custom_call_target="tpu_custom_call" | custom-call | tf_op jit(solution)/shard_map/pallas_call | solution.py:470
  222.6 0.9 copy.17
  (7 shorter events, 0.1 us)
Async XLA Ops:
  0.6 1.5 copy-start
  3.7 112.8 %copy-start.3 = (bf16[2,2,576]{2,1,0:T(2,128)(2,1)S(1)}, bf16[2,2,576]{2,1,0:T(2,128)(2,1)}, u32[]{:S(2)}) copy-start(bf16[2,2,576]{2,1,0:T(2,128)(2,1)} %param.18) | copy-start | bytes 13828
  3.7 112.8 %copy-start.2 = (bf16[2,2,128,576]{2,3,1,0:T(8,128)(2,1)S(1)}, bf16[2,2,128,576]{2,3,1,0:T(8,128)(2,1)}, u32[]{:S(2)}) copy-start(bf16[2,2,128,576]{2,3,1,0:T(8,128)(2,1)} %param.17) | copy-start | bytes 1769476
  116.5 3.2 %copy-start.1 = (bf16[2,3072,576]{2,1,0:T(8,128)(2,1)S(1)}, bf16[2,3072,576]{2,1,0:T(8,128)(2,1)}, u32[]{:S(2)}) copy-start(bf16[2,3072,576]{2,1,0:T(8,128)(2,1)} %shard_map.131.arrived) | copy-start | bytes 21233668
  119.7 11.1 %copy-start.4 = (bf16[896]{0:T(1024)(128)(2,1)S(1)}, bf16[896]{0:T(1024)(128)(2,1)}, u32[]{:S(2)}) copy-start(bf16[896]{0:T(1024)(128)(2,1)} %param.22) | copy-start | bytes 5380

commit v5 on v4

--- a/solution.py
+++ b/solution.py
@@ -21,13 +21,16 @@
     lax.fori_loop(low, high, body, 0)
 
 
-def move_kernel(n_dp, n_tp, chunks, picked, cache, out, loaded, stage, mid, load_sem, own_sem, send1, recv1, send2, recv2):
-    group_req, piece, _ = loaded.shape
-    per_pair = group_req // n_dp
-    per_dev = group_req // n_tp
+def move_kernel(
+    n_dp, n_tp, chunks, ahead, picked, cache, out, loaded, stage, mid, load_sem, own_sem, send1, recv1, send2, recv2
+):
+    group_req, piece, width = loaded.shape
     rows = piece // chunks
+    rank = (stage.shape[2] - 128) // 2
+    pairs = n_tp // n_dp
     g = lax.axis_index("dp")
     c = lax.axis_index("tp")
+
     load = pltpu.make_async_copy(cache, loaded, load_sem)
     load.start()
     barrier = pltpu.get_barrier_semaphore()
@@ -43,22 +46,27 @@
     pl.semaphore_wait(barrier, n_dp + n_tp - 2)
     load.wait()
 
-    def sort(i):
-        stage[i] = loaded[picked[i]]
-
-    loop(0, group_req, sort)
-
-    def keep(i):
-        mid[per_pair * g + i] = stage[per_pair * g + i]
-
-    loop(0, per_pair, keep)
+    def sort(q):
+        part = pl.ds(q * rows, rows)
+
+        def one(i):
+            first = picked[2 * i]
+            second = picked[2 * i + 1]
+            stage[i, part, 0:rank] = loaded[first, part, 0:rank]
+            stage[i, part, rank : 2 * rank] = loaded[second, part, 0:rank]
+            tails = [loaded[first, part, rank:width], loaded[second, part, rank:width]]
+            stage[i, part, 2 * rank :] = jnp.concatenate(tails, axis=1)
+
+        loop(0, n_tp, one)
+        for n in range(pairs):
+            mid[pairs * g + n, part] = stage[pairs * g + n, part]
 
     def over_dp(q, i, from_group):
         to_group = lax.rem(g + i, n_dp)
         part = pl.ds(q * rows, rows)
         return pltpu.make_async_remote_copy(
-            src_ref=stage.at[pl.ds(per_pair * to_group, per_pair), part],
-            dst_ref=mid.at[pl.ds(per_pair * from_group, per_pair), part],
+            src_ref=stage.at[pl.ds(pairs * to_group, pairs), part],
+            dst_ref=mid.at[pl.ds(pairs * from_group, pairs), part],
             send_sem=send1.at[q, to_group],
             recv_sem=recv1.at[q, from_group],
             device_id=(to_group, c),
@@ -68,8 +76,8 @@
     def over_tp(q, i, from_column):
         to_column = lax.rem(c + i, n_tp)
         return pltpu.make_async_remote_copy(
-            src_ref=mid.at[pl.ds(per_dev * to_column, per_dev), pl.ds(q * rows, rows)],
-            dst_ref=out.at[:, pl.ds(from_column * piece + q * rows, rows)],
+            src_ref=mid.at[to_column, pl.ds(q * rows, rows)],
+            dst_ref=out.at[pl.ds(from_column * piece + q * rows, rows)],
             send_sem=send2.at[q, to_column],
             recv_sem=recv2.at[q, from_column],
             device_id=(g, to_column),
@@ -78,14 +86,12 @@
 
     def own(q):
         return pltpu.make_async_copy(
-            mid.at[pl.ds(per_dev * c, per_dev), pl.ds(q * rows, rows)],
-            out.at[:, pl.ds(c * piece + q * rows, rows)],
-            own_sem.at[q],
+            mid.at[c, pl.ds(q * rows, rows)], out.at[pl.ds(c * piece + q * rows, rows)], own_sem.at[q]
         )
 
-    ahead = 2
     for q in range(chunks + 1):
         if q < chunks:
+            sort(q)
             if q >= ahead:
                 loop(1, n_dp, lambda i: over_dp(q - ahead, i, g).wait_send())
             loop(1, n_dp, lambda i: over_dp(q, i, g).start())
@@ -101,19 +107,19 @@
         own(q).wait()
 
 
-def move(picked, old_cache, n_dp, n_tp):
+def move(picked, old_cache, n_dp, n_tp, chunks=12, ahead=2):
     group_req, piece, width = old_cache.shape
-    chunks = 12
+    packed = (n_tp, piece, 2 * width)
     sems = pltpu.SemaphoreType.DMA
     return pl.pallas_call(
-        functools.partial(move_kernel, n_dp, n_tp, chunks),
-        out_shape=jax.ShapeDtypeStruct((group_req // n_tp, piece * n_tp, width), old_cache.dtype),
+        functools.partial(move_kernel, n_dp, n_tp, chunks, ahead),
+        out_shape=jax.ShapeDtypeStruct((piece * n_tp, 2 * width), old_cache.dtype),
         in_specs=[pl.BlockSpec(memory_space=pltpu.SMEM), pl.BlockSpec(memory_space=pl.ANY)],
         out_specs=pl.BlockSpec(memory_space=pl.ANY),
         scratch_shapes=[
             pltpu.VMEM(old_cache.shape, old_cache.dtype),
-            pltpu.VMEM(old_cache.shape, old_cache.dtype),
-            pltpu.VMEM(old_cache.shape, old_cache.dtype),
+            pltpu.VMEM(packed, old_cache.dtype),
+            pltpu.VMEM(packed, old_cache.dtype),
             sems,
             sems((chunks,)),
             sems((chunks, n_dp)),
@@ -129,49 +135,65 @@
 norm_eps = 1e-06
 
 
-def attend_kernel(lens, arrived, queries, new_latent, cache_out, lat, scores):
+def attend_kernel(lens, main, tail, queries, new_main, new_tail, cache_out, lat, scores, query):
     f32, bf16 = jnp.float32, jnp.bfloat16
     item = pl.program_id(0)
     length = lens[item]
-    context, width = arrived.shape[1:]
+    context, rank = main.shape
     heads = queries.shape[3]
     both = 2 * heads
-    kv_rank = lat.shape[2]
-    query = jnp.concatenate([queries[0, 0], queries[1, 0]], axis=1)
-    first = new_latent[0, item].astype(f32)
-    second = new_latent[1, item].astype(f32)
-    block = 256
-    row = lax.broadcasted_iota(jnp.int32, (block, width), 0)
+    query[:rank] = jnp.concatenate([queries[0, 0, :rank], queries[1, 0, :rank]], axis=1)
+    query[rank:] = jnp.zeros((128, both), bf16)
+    half = pl.multiple_of(rank + item * 64, 64)
+    query[pl.ds(half, 64)] = jnp.concatenate([queries[0, 0, rank:], queries[1, 0, rank:]], axis=1)
+    block = context // 2
+    row = lax.broadcasted_iota(jnp.int32, (block, rank), 0)
+    tail_row = lax.broadcasted_iota(jnp.int32, (block, 128), 0)
+    tail_length = jnp.where(lax.broadcasted_iota(jnp.int32, (block, 128), 1) < 64, lens[0], lens[1])
     place = lax.broadcasted_iota(jnp.int32, (block, both), 0)
     last = length + lax.broadcasted_iota(jnp.int32, (block, both), 1) // heads
+
+    def fill(old, position, size, first, second):
+        new = jnp.where(position == size, first.astype(f32), jnp.where(position == size + 1, second.astype(f32), 0.0))
+        return jnp.where(position < size, old.astype(f32), new).astype(bf16)
 
     def score(i, top):
         start = pl.multiple_of(i * block, block)
         rows = pl.ds(start, block)
-        position = row + start
-        keys = arrived[0, rows].astype(f32)
-        keys = jnp.where(position < length, keys, jnp.where(position == length, first, jnp.where(position == length + 1, second, 0.0)))
-        keys = keys.astype(bf16)
-        cache_out[0, :, rows] = keys.T
-        raw = jnp.dot(keys, query, preferred_element_type=f32) * score_scale
-        raw = jnp.where(place + start <= last, raw, -jnp.inf)
+        keys = fill(main[rows], row + start, length, new_main[0, item], new_main[1, item])
+        tails = fill(tail[rows], tail_row + start, tail_length, new_tail[0], new_tail[1])
+        cache_out[0, :rank, rows] = keys.T
+        tails_t = tails.T
+
+        @pl.when(item == 0)
+        def _():
+            cache_out[0, rank:, rows] = tails_t[:64]
+
+        @pl.when(item == 1)
+        def _():
+            cache_out[0, rank:, rows] = tails_t[64:]
+
+        both_parts = jnp.concatenate([keys, tails], axis=1)
+        raw = jnp.dot(both_parts, query[...], preferred_element_type=f32)
+        raw = jnp.where(place + start <= last, raw * score_scale, -jnp.inf)
         scores[rows] = raw
         return jnp.maximum(top, jnp.max(raw, axis=0, keepdims=True))
 
     top = lax.fori_loop(0, context // block, score, jnp.full((1, both), -jnp.inf, f32))
     exponent = jnp.exp(scores[...] - top)
     total = jnp.sum(exponent, axis=0, keepdims=True)
-    mixed_t = jnp.dot(cache_out[0, :kv_rank], exponent.astype(bf16), preferred_element_type=f32)
+    mixed_t = jnp.dot(cache_out[0, :rank], exponent.astype(bf16), preferred_element_type=f32)
     mixed = (mixed_t / total).T
-    mixed = mixed.reshape(2, lat.shape[0], -1, kv_rank)
+    mixed = mixed.reshape(2, lat.shape[0], -1, rank)
     mixed = jnp.concatenate([mixed[0], mixed[1]], axis=1).astype(bf16)
     lat[:, pl.ds(pl.multiple_of(item * 16, 16), 16)] = mixed
 
 
 def attend(my_lengths, arrived, queries, new_latent, n_tp, kv_rank):
-    items, context, width = arrived.shape
-    steps, _, heads, _ = queries.shape
+    context = arrived.shape[0]
+    steps, items, heads, width = queries.shape
     bf16 = jnp.bfloat16
+    new_tail = new_latent[:, :, kv_rank:].reshape(steps, 1, -1)
     flipped, latents = pl.pallas_call(
         attend_kernel,
         grid=(items,),
@@ -181,9 +203,11 @@
         ),
         in_specs=[
             pl.BlockSpec(memory_space=pltpu.SMEM),
-            pl.BlockSpec((1, context, width), lambda i: (i, 0, 0)),
+            pl.BlockSpec((context, kv_rank), lambda i: (0, i)),
+            pl.BlockSpec((context, 128), lambda i: (0, 2 * kv_rank // 128)),
             pl.BlockSpec((steps, 1, width, heads), lambda i: (0, i, 0, 0)),
-            pl.BlockSpec((steps, items, 1, width), lambda i: (0, 0, 0, 0)),
+            pl.BlockSpec((steps, items, 1, kv_rank), lambda i: (0, 0, 0, 0)),
+            pl.BlockSpec((steps, 1, 128), lambda i: (0, 0, 0)),
         ],
         out_specs=(
             pl.BlockSpec((1, width, context), lambda i: (i, 0, 0)),
@@ -191,10 +215,12 @@
         ),
         scratch_shapes=[
             pltpu.VMEM((context, steps * heads), jnp.float32),
+            pltpu.VMEM((kv_rank + 128, steps * heads), bf16),
         ],
         compiler_params=pltpu.CompilerParams(vmem_limit_bytes=40 * 2**20),
-    )(my_lengths, arrived, queries.transpose(0, 1, 3, 2), new_latent[:, :, None, :])
+    )(my_lengths, arrived, arrived, queries.transpose(0, 1, 3, 2), new_latent[:, :, None, :kv_rank], new_tail)
     return flipped.transpose(0, 2, 1), latents
+
 
 def dense_kernel(
     lat,

time: 224 us -> 215 us (0.960)
  Pallas kernels: 216 us -> 207 us
    pallas_call x1, Pallas kernels: 113 us -> 104 us  [move(): pl.pallas_call(functools.partial(move_kernel, n_dp, n_tp, chunks, ahead),...]
where the time goes in v5:
time: 215 us; the launch traced here: 214 us
  Pallas kernels  207 us (96%)
  local copies, waits for them, and re-layouts  5.42 us (3%)
    pallas_call x1, Pallas kernels, move(): pl.pallas_call(functools.partial(move_kernel, n_dp, n_tp, chunks, ahead),...  104 us
    pallas_call x1, Pallas kernels, dense(): pl.pallas_call(dense_kernel, out_shape=jax.ShapeDtypeStruct((steps, 16, 1...  91.9 us
    pallas_call x1, Pallas kernels, attend(): pl.pallas_call(attend_kernel, grid=(items,), out_shape=(jax.ShapeDtypeStr...  11 us

profile of v5, /device:TPU:1, one launch (start us, length us, event | category | flops | bytes accessed | tf_op | source)
XLA Modules:
  0.0 214.4 jit_solution(1721890520294396788)
XLA Ops:
  0.6 0.0 copy-start
  0.7 0.8 select_reduce_fusion
  1.5 0.6 gather_fusion
  2.1 0.0 copy-done
  2.1 0.6 gather_fusion.1
  2.8 0.7 fusion.1
  3.5 0.1 dynamic_slice.3
  3.6 0.1 select_reduce_fusion.1.picked
  3.7 0.0 copy-start.3
  3.7 0.0 slice-start
  3.7 0.0 copy-start.2
  3.7 103.6 %shard_map.131.main.tail = bf16[3072,1152]{1,0:T(8,128)(2,1)} custom-call(s32[32]{0:T(128)S(1)} %select_reduce_fusion.1.picked, bf16[32,192,576]{2,1,0:T(8,128)(2,1)} %cache.1), custom_call_target="tpu_custom_call" | custom-call | tf_op jit(solution)/shard_map/pallas_call | solution.py:114
  107.4 0.0 copy-done.3
  107.4 0.0 slice-done
  107.4 0.1 reshape.46.new_tail
  107.5 0.0 copy-done.2
  107.5 0.0 copy-start.1
  107.5 3.0 %copy-done.1 = bf16[3072,1152]{1,0:T(8,128)(2,1)S(1)} copy-done((bf16[3072,1152]{1,0:T(8,128)(2,1)S(1)}, bf16[3072,1152]{1,0:T(8,128)(2,1)}, u32[]{:S(2)}) %copy-start.1) | copy-done | bytes 7077912
  110.5 0.0 copy-start.4
  110.5 11.0 %shard_map.132 = (bf16[2,576,3072]{2,1,0:T(8,128)(2,1)}, bf16[16,32,512]{2,1,0:T(8,128)(2,1)S(1)}) custom-call(s32[2]{0:T(128)S(1)} %and_select_fusion.lens, bf16[3072,1152]{1,0:T(8,128)(2,1)S(1)} %copy-done.1, bf16[3072,1152]{1,0:T(8,128)(2,1)S(1)} %copy-done.1, bf16[2,2,576,128]{3,2,1,0:T(8,128)(2,1)S(1)} %bitcast.7, ...), custom_call_target="tpu_custom_call" | custom-call | tf_op jit(solution)/shard_map/pallas_call | solution.py:197
  121.5 0.0 copy-done.4
  121.5 91.9 %shard_map.133 = bf16[2,16,16,896]{3,2,1,0:T(8,128)(2,1)S(1)} custom-call(bf16[16,32,512]{2,1,0:T(8,128)(2,1)S(1)} %get-tuple-element.6.lat, bf16[8,512,128]{2,1,0:T(8,128)(2,1)} %value_up.1, bf16[2,16,16,896]{3,2,1,0:T(8,128)(2,1)} %bitcast.8, f32[1,896]{1,0:T(1,128)S(1)} %reshape.23.gain, bf16[1024,896]{1,0:T(8,128)(2,1)} %w_out.1, ...), custom_call_target="tpu_custom_call" | custom-call | tf_op jit(solution)/shard_map/pallas_call | solution.py:496
  213.4 0.9 copy.19
  (8 shorter events, 0.1 us)
Async XLA Ops:
  0.6 1.5 copy-start
  3.7 103.7 %copy-start.3 = (bf16[2,2,576]{2,1,0:T(2,128)(2,1)S(1)}, bf16[2,2,576]{2,1,0:T(2,128)(2,1)}, u32[]{:S(2)}) copy-start(bf16[2,2,576]{2,1,0:T(2,128)(2,1)} %param.18) | copy-start | bytes 13828
  3.7 103.7 %slice-start = ((bf16[2,2,576]{2,1,0:T(2,128)(2,1)}), bf16[2,2,64]{2,1,0:T(2,128)(2,1)S(1)}, s32[]{:S(2)}) async-start(bf16[2,2,576]{2,1,0:T(2,128)(2,1)} %param.18), calls=%async_computation | async-start | bytes 2048 | tf_op jit(solution)/shard_map/slice | solution.py:196
  3.7 103.8 %copy-start.2 = (bf16[2,2,128,576]{2,3,1,0:T(8,128)(2,1)S(1)}, bf16[2,2,128,576]{2,3,1,0:T(8,128)(2,1)}, u32[]{:S(2)}) copy-start(bf16[2,2,128,576]{2,3,1,0:T(8,128)(2,1)} %param.17) | copy-start | bytes 1769476
  107.5 3.0 %copy-start.1 = (bf16[3072,1152]{1,0:T(8,128)(2,1)S(1)}, bf16[3072,1152]{1,0:T(8,128)(2,1)}, u32[]{:S(2)}) copy-start(bf16[3072,1152]{1,0:T(8,128)(2,1)} %shard_map.131.main.tail) | copy-start | bytes 21233668
  110.5 11.0 %copy-start.4 = (bf16[896]{0:T(1024)(128)(2,1)S(1)}, bf16[896]{0:T(1024)(128)(2,1)}, u32[]{:S(2)}) copy-start(bf16[896]{0:T(1024)(128)(2,1)} %param.22) | copy-start | bytes 5380

commit v6 on v5

--- a/solution.py
+++ b/solution.py
@@ -217,7 +217,7 @@
             pltpu.VMEM((context, steps * heads), jnp.float32),
             pltpu.VMEM((kv_rank + 128, steps * heads), bf16),
         ],
-        compiler_params=pltpu.CompilerParams(vmem_limit_bytes=40 * 2**20),
+        compiler_params=pltpu.CompilerParams(vmem_limit_bytes=58 * 2**20),
     )(my_lengths, arrived, arrived, queries.transpose(0, 1, 3, 2), new_latent[:, :, None, :kv_rank], new_tail)
     return flipped.transpose(0, 2, 1), latents
 
@@ -566,21 +566,14 @@
     req_total = new_slot.shape[0]
     kv_rank = value_up_weight.shape[1]
     everyone = jnp.arange(req_total, dtype=jnp.int32)
-    new_group = new_slot // group_req
-    pair_rank = new_slot % group_req - everyone // group_req * per_pair
-    my_targets = lax.dynamic_slice_in_dim(
-        new_group * per_pair + pair_rank, my_group * group_req, group_req
-    )
-    target_places = jnp.arange(group_req, dtype=jnp.int32)
+    order = jnp.arange(group_req, dtype=jnp.int32)
+    out_slots = order // per_pair * group_req + my_group * per_pair + order % per_pair
     picked = jnp.sum(
-        jnp.where(my_targets[None, :] == target_places[:, None], target_places[None, :], 0), axis=1
+        jnp.where(new_slot[None, :] == out_slots[:, None], everyone[None, :] % group_req, 0), axis=1
     )
     arrived = move(picked, old_cache, dp_count, tp_count)
-    source = jnp.sum(
-        jnp.where(new_slot[None, :] == everyone[:, None], everyone[None, :], 0), axis=1
-    )
     my_slots = (my_group * tp_count + my_column) * req_dev + jnp.arange(req_dev, dtype=jnp.int32)
-    my_lengths = jnp.take(lengths, jnp.take(source, my_slots))
+    my_lengths = jnp.sum(jnp.where(new_slot[None, :] == my_slots[:, None], lengths[None, :], 0), axis=1)
     new_cache, latents = attend(my_lengths, arrived, queries, new_latent, tp_count, kv_rank)
     gain = norm_gain.astype(jnp.float32)[None, :]
     layer_out = dense(latents, value_up_weight, hidden, gain, w_out, w_gate, w_up, w_down)

time: 215 us -> 215 us (level)
  local copies, waits for them, and re-layouts: 5.42 us -> 3.26 us
where the time goes in v6:
time: 215 us; the launch traced here: 214 us
  Pallas kernels  208 us (97%)
  local copies, waits for them, and re-layouts  3.26 us (2%)
  other arithmetic  2.34 us (1%)
    pallas_call x1, Pallas kernels, move(): pl.pallas_call(functools.partial(move_kernel, n_dp, n_tp, chunks, ahead),...  104 us
    pallas_call x1, Pallas kernels, dense(): pl.pallas_call(dense_kernel, out_shape=jax.ShapeDtypeStruct((steps, 16, 1...  91.9 us
    pallas_call x1, Pallas kernels, attend(): pl.pallas_call(attend_kernel, grid=(items,), out_shape=(jax.ShapeDtypeStr...  12.6 us

profile of v6, /device:TPU:1, one launch (start us, length us, event | category | flops | bytes accessed | tf_op | source)
XLA Modules:
  0.0 214.4 jit_solution(1156690634395183819)
XLA Ops:
  0.6 1.5 fusion.lens
  2.1 0.9 select_reduce_fusion.picked
  3.0 0.0 copy-start.1
  3.0 0.0 slice-start
  3.0 103.6 %shard_map.131.main.tail = bf16[3072,1152]{1,0:T(8,128)(2,1)} custom-call(s32[32]{0:T(128)S(1)} %select_reduce_fusion.picked, bf16[32,192,576]{2,1,0:T(8,128)(2,1)} %cache.1), custom_call_target="tpu_custom_call" | custom-call | tf_op jit(solution)/shard_map/pallas_call | solution.py:114
  106.6 0.0 copy-done.1
  106.7 0.6 copy.16.new_main
  107.3 0.0 slice-done
  107.3 0.7 reshape.61.new_tail
  107.9 0.0 copy-start.2
  107.9 12.6 %shard_map.132 = (bf16[2,576,3072]{2,1,0:T(8,128)(2,1)}, bf16[16,32,512]{2,1,0:T(8,128)(2,1)}) custom-call(s32[2]{0:T(128)} %fusion.lens, bf16[3072,1152]{1,0:T(8,128)(2,1)} %shard_map.131.main.tail, bf16[3072,1152]{1,0:T(8,128)(2,1)} %shard_map.131.main.tail, bf16[2,2,576,128]{3,2,1,0:T(8,128)(2,1)} %bitcast.8, bf16[2,2,1,512]{3,2,1,0:T(2,128)(2,1)} %copy.16.new_main, ...), custom_call_target="tpu_custom_call" | custom-call | tf_op jit(solution)/shard_map/pallas_call | solution.py:197
  120.6 0.0 copy-done.2
  120.6 0.0 copy-start
  120.6 1.0 copy-done
  121.6 91.9 %shard_map.133 = bf16[2,16,16,896]{3,2,1,0:T(8,128)(2,1)S(1)} custom-call(bf16[16,32,512]{2,1,0:T(8,128)(2,1)S(1)} %copy-done, bf16[8,512,128]{2,1,0:T(8,128)(2,1)} %value_up.1, bf16[2,16,16,896]{3,2,1,0:T(8,128)(2,1)} %bitcast.7, f32[1,896]{1,0:T(1,128)S(1)} %reshape.60.gain, bf16[1024,896]{1,0:T(8,128)(2,1)} %w_out.1, bf16[896,1152]{1,0:T(8,128)(2,1)} %w_gate.1, ...), custom_call_target="tpu_custom_call" | custom-call | tf_op jit(solution)/shard_map/pallas_call | solution.py:496
  213.5 0.9 copy.19
  (5 shorter events, 0.0 us)
Async XLA Ops:
  3.0 103.7 %copy-start.1 = (bf16[2,2,576]{2,1,0:T(2,128)(2,1)S(1)}, bf16[2,2,576]{2,1,0:T(2,128)(2,1)}, u32[]{:S(2)}) copy-start(bf16[2,2,576]{2,1,0:T(2,128)(2,1)} %param.16) | copy-start | bytes 13828
  3.0 104.3 %slice-start = ((bf16[2,2,576]{2,1,0:T(2,128)(2,1)}), bf16[2,2,64]{2,1,0:T(2,128)(2,1)S(1)}, s32[]{:S(2)}) async-start(bf16[2,2,576]{2,1,0:T(2,128)(2,1)} %param.16), calls=%async_computation | async-start | bytes 2048 | tf_op jit(solution)/shard_map/slice | solution.py:196
  107.9 12.6 %copy-start.2 = (bf16[896]{0:T(1024)(128)(2,1)S(1)}, bf16[896]{0:T(1024)(128)(2,1)}, u32[]{:S(2)}) copy-start(bf16[896]{0:T(1024)(128)(2,1)} %param.20) | copy-start | bytes 5380
  120.6 1.0 copy-start

commit v7 on v6

--- a/solution.py
+++ b/solution.py
@@ -217,7 +217,7 @@
             pltpu.VMEM((context, steps * heads), jnp.float32),
             pltpu.VMEM((kv_rank + 128, steps * heads), bf16),
         ],
-        compiler_params=pltpu.CompilerParams(vmem_limit_bytes=58 * 2**20),
+        compiler_params=pltpu.CompilerParams(vmem_limit_bytes=40 * 2**20),
     )(my_lengths, arrived, arrived, queries.transpose(0, 1, 3, 2), new_latent[:, :, None, :kv_rank], new_tail)
     return flipped.transpose(0, 2, 1), latents
 
@@ -242,6 +242,7 @@
     xbuf,
     s3,
     r3,
+    t3,
     after,
     ybuf,
     gu,
@@ -345,33 +346,75 @@
         loop(1, 4, lambda i: gather_ring(buf, ss, rs, s, i, g).wait_send())
         loop(0, 4, lambda i: gather_pair(buf, ss, rs, s, i, g, g).wait_send())
 
-    def scatter_copy(ss, rs, s, i, source):
-        to = lax.rem(c + i, 16)
-        return remote(s3.at[s, block_of(to)], r3.at[s, source], ss.at[s, to], rs.at[s, source], g, to)
+    def shift(s, one, two):
+        over_x, over_z = one + s * (two - one), two + s * (one - two)
+        return 4 * lax.rem(z + over_z, 4) + lax.rem(x + over_x, 4)
+
+    def scatter_one(ss, rs, s, one, two):
+        return remote(
+            s3.at[s, block_of(shift(s, one, two))],
+            r3.at[s, 4 * one + two],
+            ss.at[s, 4 * one + two],
+            rs.at[s, 4 * one + two],
+            g,
+            shift(s, one, 0),
+        )
+
+    def scatter_two(ss, rs, s, two):
+        return remote(t3.at[s, two], r3.at[s, two], ss.at[s, two], rs.at[s, two], g, shift(s, 0, two))
 
     def scatter(value, ss, rs, s):
         s3[s] = value.reshape(16, 16, value.shape[1]).astype(bf16)
-        loop(1, 16, lambda i: scatter_copy(ss, rs, s, i, c).start())
+        loop(0, 12, lambda n: scatter_one(ss, rs, s, 1 + n // 4, lax.rem(n + 1, 4)).start())
+
+    def first_sum(ss, rs, s, two):
+        loop(1, 4, lambda one: scatter_one(ss, rs, s, one, two).wait_recv())
+        total = s3[s, block_of(shift(s, 0, two))].astype(f32)
+        for one in range(1, 4):
+            total = total + r3[s, 4 * one + two].astype(f32)
+        return total
+
+    def scatter_mid(ss, rs, s):
+        def send(two):
+            t3[s, two] = first_sum(ss, rs, s, two).astype(bf16)
+            scatter_two(ss, rs, s, two).start()
+
+        loop(1, 4, send)
 
     def scatter_sum(ss, rs, s, first):
-        r3[s, c] = s3[s, mine]
-        loop(1, 16, lambda i: scatter_copy(ss, rs, s, i, lax.rem(c + 16 - i, 16)).wait_recv())
-        total = first + jnp.sum(r3[s].astype(f32), axis=0)
-        loop(1, 16, lambda i: scatter_copy(ss, rs, s, i, c).wait_send())
+        total = first + first_sum(ss, rs, s, 0)
+        loop(1, 4, lambda two: scatter_two(ss, rs, s, two).wait_recv())
+        for two in range(1, 4):
+            total = total + r3[s, two].astype(f32)
+        loop(0, 12, lambda n: scatter_one(ss, rs, s, 1 + n // 4, lax.rem(n, 4)).wait_send())
+        loop(1, 4, lambda two: scatter_two(ss, rs, s, two).wait_send())
         return total
 
-    def spread(buf, ss, rs, s, i, source):
-        to = lax.rem(c + i, 16)
-        return remote(buf.at[s, mine], buf.at[s, block_of(source)], ss.at[s, to], rs.at[s, source], g, to)
+    def spread(buf, ss, rs, s, slot, source, to):
+        block = block_of(source)
+        return remote(buf.at[s, block], buf.at[s, block], ss.at[s, slot], rs.at[s, source], g, to)
 
     def spread_start(buf, ss, rs, s):
-        loop(1, 16, lambda i: spread(buf, ss, rs, s, i, c).start())
+        loop(1, 4, lambda i: spread(buf, ss, rs, s, i, c, shift(s, i, 0)).start())
+        loop(1, 4, lambda j: spread(buf, ss, rs, s, 3 + j, c, shift(s, 0, j)).start())
+
+    def spread_mid(buf, ss, rs, s):
+        def forward(i):
+            source = shift(s, 4 - i, 0)
+            spread(buf, ss, rs, s, i, source, source).wait_recv()
+            loop(1, 4, lambda j: spread(buf, ss, rs, s, 3 + 3 * i + j, source, shift(s, 0, j)).start())
+
+        loop(1, 4, forward)
 
     def spread_wait(buf, ss, rs, s):
-        loop(1, 16, lambda i: spread(buf, ss, rs, s, i, lax.rem(c + 16 - i, 16)).wait_recv())
+        def arrive(n):
+            source = shift(s, lax.rem(4 - n // 3, 4), 3 - lax.rem(n, 3))
+            spread(buf, ss, rs, s, 0, source, source).wait_recv()
+
+        loop(0, 12, arrive)
 
     def spread_end(buf, ss, rs, s):
-        loop(1, 16, lambda i: spread(buf, ss, rs, s, i, c).wait_send())
+        loop(1, 16, lambda slot: spread(buf, ss, rs, s, slot, c, shift(s, 1, 0)).wait_send())
 
     loop(0, 2, lambda s: gather_start(xbuf, x_ss, x_rs, s))
     loads[1].wait()
@@ -382,6 +425,7 @@
         scatter(jnp.dot(rows, wout_v[...], preferred_element_type=f32), s3_ss, s3_rs, s)
 
     loop(0, 2, out_stage)
+    loop(0, 2, lambda s: scatter_mid(s3_ss, s3_rs, s))
 
     def after_stage(s):
         after[s] = scatter_sum(s3_ss, s3_rs, s, hidden[s, mine].astype(f32))
@@ -389,6 +433,7 @@
         spread_start(ybuf, y_ss, y_rs, s)
 
     loop(0, 2, after_stage)
+    loop(0, 2, lambda s: spread_mid(ybuf, y_ss, y_rs, s))
     loads[2].wait()
     loads[3].wait()
     lane = lax.broadcasted_iota(jnp.int32, (32, 128), 1)
@@ -467,12 +512,14 @@
         scatter(jnp.dot(rows, wdown_v[...], preferred_element_type=f32), s7_ss, s7_rs, s)
 
     loop(0, 2, down_stage)
+    loop(0, 2, lambda s: scatter_mid(s7_ss, s7_rs, s))
 
     def result_stage(s):
         out[s, mine] = scatter_sum(s7_ss, s7_rs, s, after[s]).astype(bf16)
         spread_start(out, o_ss, o_rs, s)
 
     loop(0, 2, result_stage)
+    loop(0, 2, lambda s: spread_mid(out, o_ss, o_rs, s))
     loop(1, 16, lambda i: lat_copy(i, c).wait_send())
 
     def end_stage(s):
@@ -509,6 +556,7 @@
             vmem((2, 8, 32, w_out.shape[0]), bf16),
             vmem((2, 16, 16, cols), bf16),
             vmem((2, 16, 16, cols), bf16),
+            vmem((2, 4, 16, cols), bf16),
             vmem((2, 16, cols), f32),
             vmem((2, 16, 16, cols), bf16),
             vmem((2, 4, 2, 32, 2 * ff + 128), f32),

time: 215 us -> 213 us (level)
  no operation moved by 1% of the time
where the time goes in v7:
time: 213 us
  Pallas kernels  206 us (97%)
  local copies, waits for them, and re-layouts  4.06 us (2%)
    pallas_call x1, Pallas kernels, move(): pl.pallas_call(functools.partial(move_kernel, n_dp, n_tp, chunks, ahead),...  104 us
    pallas_call x1, Pallas kernels, dense(): pl.pallas_call(dense_kernel, out_shape=jax.ShapeDtypeStruct((steps, 16, 1...  91.6 us
    pallas_call x1, Pallas kernels, attend(): pl.pallas_call(attend_kernel, grid=(items,), out_shape=(jax.ShapeDtypeStr...  11 us

profile of v7, /device:TPU:1, one launch (start us, length us, event | category | flops | bytes accessed | tf_op | source)
XLA Modules:
  0.0 212.8 jit_solution(9348482708834927721)
XLA Ops:
  0.6 0.9 fusion.lens
  1.5 0.9 select_reduce_fusion.picked
  2.4 0.0 copy-start.2
  2.4 0.0 slice-start
  2.4 0.0 copy-start.1
  2.4 103.6 %shard_map.131.main.tail = bf16[3072,1152]{1,0:T(8,128)(2,1)} custom-call(s32[32]{0:T(128)S(1)} %select_reduce_fusion.picked, bf16[32,192,576]{2,1,0:T(8,128)(2,1)} %cache.1), custom_call_target="tpu_custom_call" | custom-call | tf_op jit(solution)/shard_map/pallas_call | solution.py:114
  106.1 0.0 copy-done.2
  106.1 0.0 slice-done
  106.1 0.1 reshape.61.new_tail
  106.2 0.0 copy-done.1
  106.2 0.0 copy-start
  106.2 3.0 %copy-done = bf16[3072,1152]{1,0:T(8,128)(2,1)S(1)} copy-done((bf16[3072,1152]{1,0:T(8,128)(2,1)S(1)}, bf16[3072,1152]{1,0:T(8,128)(2,1)}, u32[]{:S(2)}) %copy-start) | copy-done | bytes 7077912
  109.2 0.0 copy-start.3
  109.2 11.0 %shard_map.132 = (bf16[2,576,3072]{2,1,0:T(8,128)(2,1)}, bf16[16,32,512]{2,1,0:T(8,128)(2,1)S(1)}) custom-call(s32[2]{0:T(128)S(1)} %fusion.lens, bf16[3072,1152]{1,0:T(8,128)(2,1)S(1)} %copy-done, bf16[3072,1152]{1,0:T(8,128)(2,1)S(1)} %copy-done, bf16[2,2,576,128]{3,2,1,0:T(8,128)(2,1)S(1)} %bitcast.7, bf16[2,2,1,512]{3,2,1,0:T(2,128)(2,1)S(1)} %copy.16.new_main, ...), custom_call_target="tpu_custom_call" | custom-call | tf_op jit(solution)/shard_map/pallas_call | solution.py:197
  120.3 0.0 copy-done.3
  120.3 91.6 %shard_map.133 = bf16[2,16,16,896]{3,2,1,0:T(8,128)(2,1)S(1)} custom-call(bf16[16,32,512]{2,1,0:T(8,128)(2,1)S(1)} %get-tuple-element.5.lat, bf16[8,512,128]{2,1,0:T(8,128)(2,1)} %value_up.1, bf16[2,16,16,896]{3,2,1,0:T(8,128)(2,1)} %bitcast.8, f32[1,896]{1,0:T(1,128)S(1)} %reshape.60.gain, bf16[1024,896]{1,0:T(8,128)(2,1)} %w_out.1, ...), custom_call_target="tpu_custom_call" | custom-call | tf_op jit(solution)/shard_map/pallas_call | solution.py:543
  211.9 0.9 copy.19
  (6 shorter events, 0.0 us)
Async XLA Ops:
  2.4 103.7 %copy-start.2 = (bf16[2,2,576]{2,1,0:T(2,128)(2,1)S(1)}, bf16[2,2,576]{2,1,0:T(2,128)(2,1)}, u32[]{:S(2)}) copy-start(bf16[2,2,576]{2,1,0:T(2,128)(2,1)} %param.16) | copy-start | bytes 13828
  2.4 103.7 %slice-start = ((bf16[2,2,576]{2,1,0:T(2,128)(2,1)}), bf16[2,2,64]{2,1,0:T(2,128)(2,1)S(1)}, s32[]{:S(2)}) async-start(bf16[2,2,576]{2,1,0:T(2,128)(2,1)} %param.16), calls=%async_computation | async-start | bytes 2048 | tf_op jit(solution)/shard_map/slice | solution.py:196
  2.4 103.8 %copy-start.1 = (bf16[2,2,128,576]{2,3,1,0:T(8,128)(2,1)S(1)}, bf16[2,2,128,576]{2,3,1,0:T(8,128)(2,1)}, u32[]{:S(2)}) copy-start(bf16[2,2,128,576]{2,3,1,0:T(8,128)(2,1)} %param.15) | copy-start | bytes 1769476
  106.2 3.0 %copy-start = (bf16[3072,1152]{1,0:T(8,128)(2,1)S(1)}, bf16[3072,1152]{1,0:T(8,128)(2,1)}, u32[]{:S(2)}) copy-start(bf16[3072,1152]{1,0:T(8,128)(2,1)} %shard_map.131.main.tail) | copy-start | bytes 21233668
  109.2 11.0 %copy-start.3 = (bf16[896]{0:T(1024)(128)(2,1)S(1)}, bf16[896]{0:T(1024)(128)(2,1)}, u32[]{:S(2)}) copy-start(bf16[896]{0:T(1024)(128)(2,1)} %param.20) | copy-start | bytes 5380

commit v8 on v6

--- a/solution.py
+++ b/solution.py
@@ -217,7 +217,7 @@
             pltpu.VMEM((context, steps * heads), jnp.float32),
             pltpu.VMEM((kv_rank + 128, steps * heads), bf16),
         ],
-        compiler_params=pltpu.CompilerParams(vmem_limit_bytes=58 * 2**20),
+        compiler_params=pltpu.CompilerParams(vmem_limit_bytes=40 * 2**20),
     )(my_lengths, arrived, arrived, queries.transpose(0, 1, 3, 2), new_latent[:, :, None, :kv_rank], new_tail)
     return flipped.transpose(0, 2, 1), latents
 
@@ -305,15 +305,16 @@
 
     def lat_copy(i, source):
         to = lax.rem(c + i, 16)
-        return remote(lat.at[to], latr.at[source], lat_ss.at[to], lat_rs.at[source], g, to)
-
+        return remote(lat.at[to], latr.at[source], lat_ss, lat_rs, g, to)
+
+    lat_all = remote(lat.at[pl.ds(0, 15)], latr.at[pl.ds(0, 15)], lat_ss, lat_rs, g, lax.rem(c + 1, 16))
     loop(1, 16, lambda i: lat_copy(i, c).start())
     latr[c] = lat[c]
     row = lax.broadcasted_iota(jnp.int32, (512, 512), 0)
     col = lax.broadcasted_iota(jnp.int32, (512, 512), 1)
     wanted = ((row & 31) >> 1) * 32 + (row & 1) * 16 + ((row >> 5) & 1) * 8 + (row >> 6)
     perm[...] = jnp.where(col == wanted, 1.0, 0.0).astype(bf16)
-    loop(1, 16, lambda i: lat_copy(i, lax.rem(c + 16 - i, 16)).wait_recv())
+    lat_all.wait_recv()
     ordered = jnp.dot(perm[...], latr[...].reshape(512, 512), preferred_element_type=f32).astype(bf16)
     loads[0].wait()
     for head in range(8):
@@ -347,7 +348,11 @@
 
     def scatter_copy(ss, rs, s, i, source):
         to = lax.rem(c + i, 16)
-        return remote(s3.at[s, block_of(to)], r3.at[s, source], ss.at[s, to], rs.at[s, source], g, to)
+        return remote(s3.at[s, block_of(to)], r3.at[s, source], ss.at[s], rs.at[s], g, to)
+
+    def scatter_all(ss, rs, s):
+        part = pl.ds(0, 15)
+        return remote(s3.at[s, part], r3.at[s, part], ss.at[s], rs.at[s], g, lax.rem(c + 1, 16))
 
     def scatter(value, ss, rs, s):
         s3[s] = value.reshape(16, 16, value.shape[1]).astype(bf16)
@@ -355,23 +360,27 @@
 
     def scatter_sum(ss, rs, s, first):
         r3[s, c] = s3[s, mine]
-        loop(1, 16, lambda i: scatter_copy(ss, rs, s, i, lax.rem(c + 16 - i, 16)).wait_recv())
+        scatter_all(ss, rs, s).wait_recv()
         total = first + jnp.sum(r3[s].astype(f32), axis=0)
-        loop(1, 16, lambda i: scatter_copy(ss, rs, s, i, c).wait_send())
+        scatter_all(ss, rs, s).wait_send()
         return total
 
     def spread(buf, ss, rs, s, i, source):
         to = lax.rem(c + i, 16)
-        return remote(buf.at[s, mine], buf.at[s, block_of(source)], ss.at[s, to], rs.at[s, source], g, to)
+        return remote(buf.at[s, mine], buf.at[s, block_of(source)], ss.at[s], rs.at[s], g, to)
+
+    def spread_all(buf, ss, rs, s):
+        part = pl.ds(0, 15)
+        return remote(buf.at[s, part], buf.at[s, part], ss.at[s], rs.at[s], g, lax.rem(c + 1, 16))
 
     def spread_start(buf, ss, rs, s):
         loop(1, 16, lambda i: spread(buf, ss, rs, s, i, c).start())
 
     def spread_wait(buf, ss, rs, s):
-        loop(1, 16, lambda i: spread(buf, ss, rs, s, i, lax.rem(c + 16 - i, 16)).wait_recv())
+        spread_all(buf, ss, rs, s).wait_recv()
 
     def spread_end(buf, ss, rs, s):
-        loop(1, 16, lambda i: spread(buf, ss, rs, s, i, c).wait_send())
+        spread_all(buf, ss, rs, s).wait_send()
 
     loop(0, 2, lambda s: gather_start(xbuf, x_ss, x_rs, s))
     loads[1].wait()
@@ -473,7 +482,7 @@
         spread_start(out, o_ss, o_rs, s)
 
     loop(0, 2, result_stage)
-    loop(1, 16, lambda i: lat_copy(i, c).wait_send())
+    lat_all.wait_send()
 
     def end_stage(s):
         gather_end(xbuf, x_ss, x_rs, s)
@@ -518,24 +527,24 @@
             vmem((2, 4, 32, 2 * ff + 128), bf16),
             vmem((2, 8, 32, ff), bf16),
             sems((5,)),
-            sems((16,)),
-            sems((16,)),
+            sems,
+            sems,
             sems((2, 8)),
             sems((2, 8)),
-            sems((2, 16)),
-            sems((2, 16)),
-            sems((2, 16)),
-            sems((2, 16)),
+            sems((2,)),
+            sems((2,)),
+            sems((2,)),
+            sems((2,)),
             sems((2, 4)),
             sems((2, 4)),
             sems((2, 4)),
             sems((2, 4)),
             sems((2, 8)),
             sems((2, 8)),
-            sems((2, 16)),
-            sems((2, 16)),
-            sems((2, 16)),
-            sems((2, 16)),
+            sems((2,)),
+            sems((2,)),
+            sems((2,)),
+            sems((2,)),
         ],
         compiler_params=pltpu.CompilerParams(collective_id=1, has_side_effects=True, vmem_limit_bytes=52 * 2**20),
     )(lat, value_up, hidden.reshape(steps, 16, 16, cols), gain, w_out, w_gate, w_up, w_down)

time: 215 us -> 211 us (0.981)
  Pallas kernels: 208 us -> 204 us
where the time goes in v8:
time: 211 us
  Pallas kernels  204 us (97%)
  local copies, waits for them, and re-layouts  4.06 us (2%)
    pallas_call x1, Pallas kernels, move(): pl.pallas_call(functools.partial(move_kernel, n_dp, n_tp, chunks, ahead),...  104 us
    pallas_call x1, Pallas kernels, dense(): pl.pallas_call(dense_kernel, out_shape=jax.ShapeDtypeStruct((steps, 16, 1...  89.7 us
    pallas_call x1, Pallas kernels, attend(): pl.pallas_call(attend_kernel, grid=(items,), out_shape=(jax.ShapeDtypeStr...  11 us

profile of v8, /device:TPU:1, one launch (start us, length us, event | category | flops | bytes accessed | tf_op | source)
XLA Modules:
  0.0 210.9 jit_solution(6464851250830949699)
XLA Ops:
  0.6 0.9 fusion.lens
  1.5 0.9 select_reduce_fusion.picked
  2.4 0.0 copy-start.2
  2.4 0.0 slice-start
  2.4 0.0 copy-start.1
  2.4 103.6 %shard_map.131.main.tail = bf16[3072,1152]{1,0:T(8,128)(2,1)} custom-call(s32[32]{0:T(128)S(1)} %select_reduce_fusion.picked, bf16[32,192,576]{2,1,0:T(8,128)(2,1)} %cache.1), custom_call_target="tpu_custom_call" | custom-call | tf_op jit(solution)/shard_map/pallas_call | solution.py:114
  106.1 0.0 copy-done.2
  106.1 0.0 slice-done
  106.1 0.1 reshape.61.new_tail
  106.2 0.0 copy-done.1
  106.2 0.0 copy-start
  106.2 3.0 %copy-done = bf16[3072,1152]{1,0:T(8,128)(2,1)S(1)} copy-done((bf16[3072,1152]{1,0:T(8,128)(2,1)S(1)}, bf16[3072,1152]{1,0:T(8,128)(2,1)}, u32[]{:S(2)}) %copy-start) | copy-done | bytes 7077912
  109.2 0.0 copy-start.3
  109.2 11.0 %shard_map.132 = (bf16[2,576,3072]{2,1,0:T(8,128)(2,1)}, bf16[16,32,512]{2,1,0:T(8,128)(2,1)S(1)}) custom-call(s32[2]{0:T(128)S(1)} %fusion.lens, bf16[3072,1152]{1,0:T(8,128)(2,1)S(1)} %copy-done, bf16[3072,1152]{1,0:T(8,128)(2,1)S(1)} %copy-done, bf16[2,2,576,128]{3,2,1,0:T(8,128)(2,1)S(1)} %bitcast.7, bf16[2,2,1,512]{3,2,1,0:T(2,128)(2,1)S(1)} %copy.16.new_main, ...), custom_call_target="tpu_custom_call" | custom-call | tf_op jit(solution)/shard_map/pallas_call | solution.py:197
  120.3 0.0 copy-done.3
  120.3 89.7 %shard_map.133 = bf16[2,16,16,896]{3,2,1,0:T(8,128)(2,1)S(1)} custom-call(bf16[16,32,512]{2,1,0:T(8,128)(2,1)S(1)} %get-tuple-element.5.lat, bf16[8,512,128]{2,1,0:T(8,128)(2,1)} %value_up.1, bf16[2,16,16,896]{3,2,1,0:T(8,128)(2,1)} %bitcast.8, f32[1,896]{1,0:T(1,128)S(1)} %reshape.60.gain, bf16[1024,896]{1,0:T(8,128)(2,1)} %w_out.1, ...), custom_call_target="tpu_custom_call" | custom-call | tf_op jit(solution)/shard_map/pallas_call | solution.py:505
  210.0 0.9 copy.19
  (6 shorter events, 0.0 us)
Async XLA Ops:
  2.4 103.7 %copy-start.2 = (bf16[2,2,576]{2,1,0:T(2,128)(2,1)S(1)}, bf16[2,2,576]{2,1,0:T(2,128)(2,1)}, u32[]{:S(2)}) copy-start(bf16[2,2,576]{2,1,0:T(2,128)(2,1)} %param.16) | copy-start | bytes 13828
  2.4 103.7 %slice-start = ((bf16[2,2,576]{2,1,0:T(2,128)(2,1)}), bf16[2,2,64]{2,1,0:T(2,128)(2,1)S(1)}, s32[]{:S(2)}) async-start(bf16[2,2,576]{2,1,0:T(2,128)(2,1)} %param.16), calls=%async_computation | async-start | bytes 2048 | tf_op jit(solution)/shard_map/slice | solution.py:196
  2.4 103.8 %copy-start.1 = (bf16[2,2,128,576]{2,3,1,0:T(8,128)(2,1)S(1)}, bf16[2,2,128,576]{2,3,1,0:T(8,128)(2,1)}, u32[]{:S(2)}) copy-start(bf16[2,2,128,576]{2,3,1,0:T(8,128)(2,1)} %param.15) | copy-start | bytes 1769476
  106.2 3.0 %copy-start = (bf16[3072,1152]{1,0:T(8,128)(2,1)S(1)}, bf16[3072,1152]{1,0:T(8,128)(2,1)}, u32[]{:S(2)}) copy-start(bf16[3072,1152]{1,0:T(8,128)(2,1)} %shard_map.131.main.tail) | copy-start | bytes 21233668
  109.2 11.0 %copy-start.3 = (bf16[896]{0:T(1024)(128)(2,1)S(1)}, bf16[896]{0:T(1024)(128)(2,1)}, u32[]{:S(2)}) copy-start(bf16[896]{0:T(1024)(128)(2,1)} %param.20) | copy-start | bytes 5380

commit v9 on v8

--- a/solution.py
+++ b/solution.py
@@ -67,8 +67,8 @@
         return pltpu.make_async_remote_copy(
             src_ref=stage.at[pl.ds(pairs * to_group, pairs), part],
             dst_ref=mid.at[pl.ds(pairs * from_group, pairs), part],
-            send_sem=send1.at[q, to_group],
-            recv_sem=recv1.at[q, from_group],
+            send_sem=send1.at[q],
+            recv_sem=recv1.at[q],
             device_id=(to_group, c),
             device_id_type=MESH,
         )
@@ -78,9 +78,31 @@
         return pltpu.make_async_remote_copy(
             src_ref=mid.at[to_column, pl.ds(q * rows, rows)],
             dst_ref=out.at[pl.ds(from_column * piece + q * rows, rows)],
-            send_sem=send2.at[q, to_column],
-            recv_sem=recv2.at[q, from_column],
+            send_sem=send2.at[q],
+            recv_sem=recv2.at[q],
             device_id=(g, to_column),
+            device_id_type=MESH,
+        )
+
+    def all_dp(q):
+        part = (pl.ds(0, pairs * (n_dp - 1)), pl.ds(q * rows, rows))
+        return pltpu.make_async_remote_copy(
+            src_ref=stage.at[part],
+            dst_ref=mid.at[part],
+            send_sem=send1.at[q],
+            recv_sem=recv1.at[q],
+            device_id=(lax.rem(g + 1, n_dp), c),
+            device_id_type=MESH,
+        )
+
+    def all_tp(q):
+        part = pl.ds(0, (n_tp - 1) * rows)
+        return pltpu.make_async_remote_copy(
+            src_ref=out.at[part],
+            dst_ref=out.at[part],
+            send_sem=send2.at[q],
+            recv_sem=recv2.at[q],
+            device_id=(g, lax.rem(c + 1, n_tp)),
             device_id_type=MESH,
         )
 
@@ -93,17 +115,17 @@
         if q < chunks:
             sort(q)
             if q >= ahead:
-                loop(1, n_dp, lambda i: over_dp(q - ahead, i, g).wait_send())
+                all_dp(q - ahead).wait_send()
             loop(1, n_dp, lambda i: over_dp(q, i, g).start())
         if q >= 1:
-            loop(1, n_dp, lambda i: over_dp(q - 1, i, lax.rem(g + n_dp - i, n_dp)).wait_recv())
+            all_dp(q - 1).wait_recv()
             loop(1, n_tp, lambda i: over_tp(q - 1, i, c).start())
             own(q - 1).start()
     for q in range(chunks):
         if q >= chunks - ahead:
-            loop(1, n_dp, lambda i: over_dp(q, i, g).wait_send())
-        loop(1, n_tp, lambda i: over_tp(q, i, c).wait_send())
-        loop(1, n_tp, lambda i: over_tp(q, i, lax.rem(c + n_tp - i, n_tp)).wait_recv())
+            all_dp(q).wait_send()
+        all_tp(q).wait_send()
+        all_tp(q).wait_recv()
         own(q).wait()
 
 
@@ -122,10 +144,10 @@
             pltpu.VMEM(packed, old_cache.dtype),
             sems,
             sems((chunks,)),
-            sems((chunks, n_dp)),
-            sems((chunks, n_dp)),
-            sems((chunks, n_tp)),
-            sems((chunks, n_tp)),
+            sems((chunks,)),
+            sems((chunks,)),
+            sems((chunks,)),
+            sems((chunks,)),
         ],
         compiler_params=pltpu.CompilerParams(collective_id=0, has_side_effects=True, vmem_limit_bytes=48 * 2**20),
     )(picked, old_cache)

time: 211 us -> 206 us (0.976)
  Pallas kernels: 204 us -> 200 us
    pallas_call x1, Pallas kernels: 104 us -> 98.9 us  [move(): pl.pallas_call(functools.partial(move_kernel, n_dp, n_tp, chunks, ahead),...]
where the time goes in v9:
time: 206 us
  Pallas kernels  200 us (97%)
  local copies, waits for them, and re-layouts  4.06 us (2%)
    pallas_call x1, Pallas kernels, move(): pl.pallas_call(functools.partial(move_kernel, n_dp, n_tp, chunks, ahead),...  98.9 us
    pallas_call x1, Pallas kernels, dense(): pl.pallas_call(dense_kernel, out_shape=jax.ShapeDtypeStruct((steps, 16, 1...  89.7 us
    pallas_call x1, Pallas kernels, attend(): pl.pallas_call(attend_kernel, grid=(items,), out_shape=(jax.ShapeDtypeStr...  11 us

profile of v9, /device:TPU:1, one launch (start us, length us, event | category | flops | bytes accessed | tf_op | source)
XLA Modules:
  0.0 206.1 jit_solution(13705452868163501842)
XLA Ops:
  0.6 0.9 fusion.lens
  1.5 0.9 select_reduce_fusion.picked
  2.4 0.0 copy-start.2
  2.4 0.0 slice-start
  2.4 0.0 copy-start.1
  2.4 98.9 %shard_map.131.main.tail = bf16[3072,1152]{1,0:T(8,128)(2,1)} custom-call(s32[32]{0:T(128)S(1)} %select_reduce_fusion.picked, bf16[32,192,576]{2,1,0:T(8,128)(2,1)} %cache.1), custom_call_target="tpu_custom_call" | custom-call | tf_op jit(solution)/shard_map/pallas_call | solution.py:136
  101.3 0.0 copy-done.2
  101.4 0.0 slice-done
  101.4 0.1 reshape.61.new_tail
  101.5 0.0 copy-done.1
  101.5 0.0 copy-start
  101.5 3.0 %copy-done = bf16[3072,1152]{1,0:T(8,128)(2,1)S(1)} copy-done((bf16[3072,1152]{1,0:T(8,128)(2,1)S(1)}, bf16[3072,1152]{1,0:T(8,128)(2,1)}, u32[]{:S(2)}) %copy-start) | copy-done | bytes 7077912
  104.5 0.0 copy-start.3
  104.5 11.0 %shard_map.132 = (bf16[2,576,3072]{2,1,0:T(8,128)(2,1)}, bf16[16,32,512]{2,1,0:T(8,128)(2,1)S(1)}) custom-call(s32[2]{0:T(128)S(1)} %fusion.lens, bf16[3072,1152]{1,0:T(8,128)(2,1)S(1)} %copy-done, bf16[3072,1152]{1,0:T(8,128)(2,1)S(1)} %copy-done, bf16[2,2,576,128]{3,2,1,0:T(8,128)(2,1)S(1)} %bitcast.7, bf16[2,2,1,512]{3,2,1,0:T(2,128)(2,1)S(1)} %copy.16.new_main, ...), custom_call_target="tpu_custom_call" | custom-call | tf_op jit(solution)/shard_map/pallas_call | solution.py:219
  115.5 0.0 copy-done.3
  115.5 89.7 %shard_map.133 = bf16[2,16,16,896]{3,2,1,0:T(8,128)(2,1)S(1)} custom-call(bf16[16,32,512]{2,1,0:T(8,128)(2,1)S(1)} %get-tuple-element.5.lat, bf16[8,512,128]{2,1,0:T(8,128)(2,1)} %value_up.1, bf16[2,16,16,896]{3,2,1,0:T(8,128)(2,1)} %bitcast.8, f32[1,896]{1,0:T(1,128)S(1)} %reshape.60.gain, bf16[1024,896]{1,0:T(8,128)(2,1)} %w_out.1, ...), custom_call_target="tpu_custom_call" | custom-call | tf_op jit(solution)/shard_map/pallas_call | solution.py:527
  205.2 0.9 copy.19
  (6 shorter events, 0.0 us)
Async XLA Ops:
  2.4 98.9 %copy-start.2 = (bf16[2,2,576]{2,1,0:T(2,128)(2,1)S(1)}, bf16[2,2,576]{2,1,0:T(2,128)(2,1)}, u32[]{:S(2)}) copy-start(bf16[2,2,576]{2,1,0:T(2,128)(2,1)} %param.16) | copy-start | bytes 13828
  2.4 99.0 %slice-start = ((bf16[2,2,576]{2,1,0:T(2,128)(2,1)}), bf16[2,2,64]{2,1,0:T(2,128)(2,1)S(1)}, s32[]{:S(2)}) async-start(bf16[2,2,576]{2,1,0:T(2,128)(2,1)} %param.16), calls=%async_computation | async-start | bytes 2048 | tf_op jit(solution)/shard_map/slice | solution.py:218
  2.4 99.0 %copy-start.1 = (bf16[2,2,128,576]{2,3,1,0:T(8,128)(2,1)S(1)}, bf16[2,2,128,576]{2,3,1,0:T(8,128)(2,1)}, u32[]{:S(2)}) copy-start(bf16[2,2,128,576]{2,3,1,0:T(8,128)(2,1)} %param.15) | copy-start | bytes 1769476
  101.5 3.0 %copy-start = (bf16[3072,1152]{1,0:T(8,128)(2,1)S(1)}, bf16[3072,1152]{1,0:T(8,128)(2,1)}, u32[]{:S(2)}) copy-start(bf16[3072,1152]{1,0:T(8,128)(2,1)} %shard_map.131.main.tail) | copy-start | bytes 21233668
  104.5 11.0 %copy-start.3 = (bf16[896]{0:T(1024)(128)(2,1)S(1)}, bf16[896]{0:T(1024)(128)(2,1)}, u32[]{:S(2)}) copy-start(bf16[896]{0:T(1024)(128)(2,1)} %param.20) | copy-start | bytes 5380
